TPU v7x, 32 devices: a whole 2x2x4 slice. The times are simulated.
32 devices in a mesh: cfg: 2 (over core), tok: 4 (over z), mlp: 4 (over y, x).
Axes of the slice: x: 2, y: 2, z: 4, core: 2. Of those that a mesh axis runs over, the one named last changes fastest.
Arguments:
- hidden: bfloat16 [2, 1536, 4, 3072], P('cfg', ('tok', 'mlp')), may hold values from -6 to 6
- latents: float32 [1536, 4, 64], P(('tok', 'mlp'), None, 'cfg'), may hold values from -6 to 6
- vec: float32 [2, 4, 3072], P('cfg'), may hold values from -9 to 9
- slot_token: int32 [4, 1536], replicated, may hold values from 0 to 1535, each once within a row
- text_len: int32 [2, 4], P('cfg'), may hold values from 64 to 512, as said below
- step_index: int32 [1], replicated, may hold values from 0 to 27
- guidance: float32 [1], replicated, may hold values from 2 to 5
- w_mod: bfloat16 [3072, 15360], P(None, ('tok', 'mlp')), may hold values from -0.109375 to 0.109375
- w_qkv: bfloat16 [1, 3072, 3, 2048], P(None, 'cfg', None, 'mlp'), may hold values from -0.109375 to 0.109375
- w_mlp_in: bfloat16 [1, 3072, 12288], P(None, 'cfg', 'mlp'), may hold values from -0.109375 to 0.109375
- qk_gain: float32 [1, 2, 128], replicated, may hold values from 1.5 to 2.5
- w_attn_out: bfloat16 [1, 2048, 3072], P(None, 'mlp', 'cfg'), may hold values from -0.125 to 0.125
- w_mlp_out: bfloat16 [1, 12288, 3072], P(None, 'mlp', 'cfg'), may hold values from -0.0546875 to 0.0546875
- w_final: bfloat16 [3072, 64], replicated, may hold values from -0.109375 to 0.109375
Outputs:
- velocity: float32 [1536, 4, 64], P(('tok', 'mlp'), None, 'cfg')
- latents_next: float32 [1536, 4, 64], P(('tok', 'mlp'), None, 'cfg')
- stream_out: bfloat16 [2, 1536, 4, 3072], P('cfg', ('tok', 'mlp'))
Inputs may be any that keep to these rules, and one draw needn't show every extreme that they name: `text_len`: real text tokens of each request; its other text slots are padding; exactly one request has all 512. `slot_token`: row p lists the token held by each slot of request p: text tokens are 0 to 511, image tokens follow row by row on the 32 x 32 grid.
All inputs are finite; a program needn't handle non-finite values.
Results may differ from a plain program's by a relative error of at most 0.018.
Values may be sent and summed in bfloat16 or wider, within the bound.
No kernel may reach another device: no remote copies, remote signals or barrier semaphores. Data moves between devices by JAX's collectives and lax.ppermute only.
A program may use at most 192 MiB of HBM per device.

v0:
```python
import math

import jax
import jax.numpy as jnp
from jax import lax
from jax.sharding import PartitionSpec as P

LAYERS = 1
SIDE = 32
TXT = 512
STEPS = 28


EPSILON = 1e-06
ROPE_BASE = 10000.0
TIME_SHIFT = 3.0


def swapped(value, axis, apart):
    return lax.ppermute(value, axis, [(i, i ^ 1 << apart) for i in range(lax.axis_size(axis))])


def layer_norm(values):
    average = jnp.mean(values, axis=-1, keepdims=True)
    centred = values - average
    spread = jnp.mean(centred * centred, axis=-1, keepdims=True)
    return centred * lax.rsqrt(spread + EPSILON)


def rms_norm(values, gains):
    return values * lax.rsqrt(jnp.mean(values * values, axis=-1, keepdims=True) + EPSILON) * gains


def rope_table(tokens, head_size, text_count, side_count):
    pair_count = head_size // 2
    first_pairs = head_size // 16
    axis_pairs = (head_size - head_size // 8) // 4
    pair_index = jnp.arange(pair_count).astype(jnp.float32)
    in_rows = (pair_index >= first_pairs) & (pair_index < first_pairs + axis_pairs)
    in_cols = pair_index >= first_pairs + axis_pairs
    log_base = math.log(ROPE_BASE)
    freq_rows = jnp.where(
        in_rows, jnp.exp(-log_base * (pair_index - first_pairs) / axis_pairs), 0.0
    )
    freq_cols = jnp.where(
        in_cols, jnp.exp(-log_base * (pair_index - first_pairs - axis_pairs) / axis_pairs), 0.0
    )
    is_image = tokens >= text_count
    image_pos = jnp.where(is_image, tokens - text_count, 0)
    row_pos = (image_pos // side_count).astype(jnp.float32)
    col_pos = (image_pos % side_count).astype(jnp.float32)
    angles = row_pos[..., None] * freq_rows + col_pos[..., None] * freq_cols
    return (jnp.cos(angles), jnp.sin(angles))


def apply_rope(values, cosine, sine_table):
    even_part = values[..., 0::2]
    odd_part = values[..., 1::2]
    return jnp.concatenate(
        [even_part * cosine - odd_part * sine_table, even_part * sine_table + odd_part * cosine],
        axis=-1,
    )


def sigma_at(position, steps_total):
    remain = 1.0 - position / steps_total
    return TIME_SHIFT * remain / (1.0 + (TIME_SHIFT - 1.0) * remain)


def on_device(
    hidden,
    latents,
    vec,
    slot_token,
    text_len,
    step_index,
    guidance,
    w_mod,
    w_qkv,
    w_mlp_in,
    qk_gain,
    w_attn_out,
    w_mlp_out,
    w_final,
):
    rows_dev = hidden.shape[1]
    prompts = hidden.shape[2]
    model_width = hidden.shape[3]
    head_size = qk_gain.shape[-1]
    mlp_count = lax.axis_size("mlp")
    tile_rows = rows_dev * mlp_count
    tok_index = lax.axis_index("tok")
    mlp_index = lax.axis_index("mlp")
    half_index = lax.axis_index("cfg")
    first_half = half_index == 0
    stream = hidden[0]
    silu_vec = jax.nn.silu(vec[0]).astype(jnp.bfloat16)
    mod_part = jnp.dot(silu_vec, w_mod, preferred_element_type=jnp.float32)
    modulation = lax.all_gather(mod_part, ("tok", "mlp"), axis=1, tiled=True)
    key_valid = ((slot_token >= TXT) | (slot_token < text_len[0][:, None])).astype(jnp.float32)
    tile_tokens = lax.dynamic_slice_in_dim(slot_token, tok_index * tile_rows, tile_rows, 1).T
    cosine, sine_table = rope_table(tile_tokens, head_size, TXT, SIDE)
    shift_mod = modulation[:, 0:model_width]
    scale_mod = modulation[:, model_width : 2 * model_width]
    gate_mod = modulation[:, 2 * model_width : 3 * model_width]
    normed = (
        layer_norm(stream.astype(jnp.float32)) * (1.0 + scale_mod[None]) + shift_mod[None]
    ).astype(jnp.bfloat16)
    tile_input = lax.all_gather(normed, "mlp", axis=0, tiled=True)
    qkv_weight = w_qkv[0]
    unit_weight = w_mlp_in[0]
    qkv_cols = qkv_weight.shape[1] * qkv_weight.shape[2]
    pieces = (
        lax.all_gather(qkv_weight, "cfg", axis=0, tiled=True),
        lax.all_gather(unit_weight, "cfg", axis=0, tiled=True),
    )
    number = pieces[0].shape[0]
    qkv_piece = pieces[0].reshape(number, qkv_cols)
    qkv_pre = jnp.einsum("tpd,dk->tpk", tile_input, qkv_piece, preferred_element_type=jnp.float32)
    unit_pre = jnp.einsum("tpd,dk->tpk", tile_input, pieces[1], preferred_element_type=jnp.float32)
    heads_dev = qkv_weight.shape[2] // head_size
    projected = qkv_pre.reshape(tile_rows, prompts, 3, heads_dev, head_size)
    queries = apply_rope(
        rms_norm(projected[:, :, 0], qk_gain[0, 0]), cosine[:, :, None], sine_table[:, :, None]
    ).astype(jnp.bfloat16)
    keys_rot = apply_rope(
        rms_norm(projected[:, :, 1], qk_gain[0, 1]), cosine[:, :, None], sine_table[:, :, None]
    ).astype(jnp.bfloat16)
    values = projected[:, :, 2].astype(jnp.bfloat16)
    activation = jax.nn.gelu(unit_pre, approximate=True).astype(jnp.bfloat16)
    keys_piece = lax.all_gather(keys_rot, "tok", axis=0, tiled=True)
    values_piece = lax.all_gather(values, "tok", axis=0, tiled=True)
    scores = jnp.einsum(
        "sphe,tphe->phst", queries, keys_piece, preferred_element_type=jnp.float32
    ) / math.sqrt(head_size)
    softened = jnp.exp(scores) * key_valid[:, None, None, :]
    numerator = jnp.einsum(
        "phst,tphe->sphe",
        softened.astype(jnp.bfloat16),
        values_piece,
        preferred_element_type=jnp.float32,
    )
    numerator, denominator = (numerator, jnp.sum(softened, axis=-1))
    attended = (numerator / jnp.transpose(denominator, (2, 0, 1))[..., None]).astype(jnp.bfloat16)
    attended = attended.reshape(tile_rows, prompts, heads_dev * head_size)
    out_attn = lax.all_gather(w_attn_out[0], "cfg", axis=1, tiled=True)
    out_units = lax.all_gather(w_mlp_out[0], "cfg", axis=1, tiled=True)
    branch_out = lax.psum_scatter(
        (
            jnp.einsum("tpk,kd->tpd", attended, out_attn, preferred_element_type=jnp.float32)
            + jnp.einsum("tpk,kd->tpd", activation, out_units, preferred_element_type=jnp.float32)
        ).astype(jnp.bfloat16),
        "mlp",
        scatter_dimension=0,
        tiled=True,
    ).astype(jnp.float32)
    stream = (stream.astype(jnp.float32) + gate_mod[None] * branch_out).astype(jnp.bfloat16)
    final_lo = 3 * LAYERS * model_width
    final_shift = modulation[:, final_lo : final_lo + model_width]
    final_scale = modulation[:, final_lo + model_width : final_lo + 2 * model_width]
    final_normed = (
        layer_norm(stream.astype(jnp.float32)) * (1.0 + final_scale[None]) + final_shift[None]
    ).astype(jnp.bfloat16)
    own_first = (tok_index * mlp_count + mlp_index) * rows_dev
    own_tokens = lax.dynamic_slice_in_dim(slot_token, own_first, rows_dev, 1).T
    half_velocity = jnp.einsum(
        "rpd,dc->rpc", final_normed, w_final, preferred_element_type=jnp.float32
    )
    half_velocity = jnp.where((own_tokens >= TXT)[:, :, None], half_velocity, 0.0)
    channel_half = latents.shape[2]
    own_part = lax.dynamic_slice_in_dim(half_velocity, half_index * channel_half, channel_half, 2)
    sent_part = lax.dynamic_slice_in_dim(
        half_velocity, (1 - half_index) * channel_half, channel_half, 2
    )
    partner = swapped(sent_part, "cfg", 0)
    cond_part = jnp.where(first_half, own_part, partner)
    uncond_part = jnp.where(first_half, partner, own_part)
    velocity = uncond_part + guidance[0] * (cond_part - uncond_part)
    current = step_index[0].astype(jnp.float32)
    step_size = sigma_at(current + 1.0, STEPS) - sigma_at(current, STEPS)
    return (velocity, latents + step_size * velocity, stream[None])


def solution(mesh):
    return jax.shard_map(
        on_device,
        mesh=mesh,
        in_specs=(
            P("cfg", ("tok", "mlp"), None, None),
            P(("tok", "mlp"), None, "cfg"),
            P("cfg", None, None),
            P(),
            P("cfg", None),
            P(),
            P(),
            P(None, ("tok", "mlp")),
            P(None, "cfg", None, "mlp"),
            P(None, "cfg", "mlp"),
            P(),
            P(None, "mlp", "cfg"),
            P(None, "mlp", "cfg"),
            P(),
        ),
        out_specs=(
            P(("tok", "mlp"), None, "cfg"),
            P(("tok", "mlp"), None, "cfg"),
            P("cfg", ("tok", "mlp"), None, None),
        ),
        check_vma=False,
    )
```

profile of v0, /device:TPU:1, one launch (start us, length us, event | category | flops | bytes accessed | tf_op | source)
XLA Modules:
  0.0 609.4 jit_solution(10738498832609015918)
XLA Ops:
  7.2 6.7 %copy.33 = bf16[1,1536,3,512]{1,3,2,0:T(8,128)(2,1)} copy(bf16[1,1536,3,512]{3,1,2,0:T(8,128)(2,1)} %param.22) | data formatting | bytes 9437184 | tf_op args[8]
  14.7 4.3 convolution_bitcast_fusion
  19.0 35.9 %all-gather.5 = f32[16,960,4]{1,2,0:T(4,128)S(1)} all-gather(f32[1,960,4]{1,2,0:T(4,128)S(1)} %convolution_bitcast_fusion), channel_id=1, replica_groups=mesh['cfg'=2,'tok'=4,'mlp'=4] {'tok','mlp'}, dimensions={0}, use_global_device_ids=true | all-gather | bytes 261120 | tf_op jit(solution)/shard_map/all_gather | solution.py:99
  57.7 2.8 fusion.39
  65.5 94.6 %all-gather.14.cloned.1.call-done = bf16[384,4,3072]{2,0,1:T(8,128)(2,1)} async-done(((bf16[96,4,3072]{2,0,1:T(8,128)(2,1)}), bf16[384,4,3072]{2,0,1:T(8,128)(2,1)}) %all-gather.14.cloned.1.call-update) | async-done | bytes 9437200 | tf_op jit(solution)/shard_map/all_gather | solution.py:109
  160.1 22.0 %fusion.19 = f32[384,4,3,4,128]{0,4,3,2,1:T(8,128)S(1)} fusion(bf16[3,4,128,3072,1]{3,2,1,0,4:T(8,128)(2,1)} %bitcast.146, bf16[384,4,3072]{2,0,1:T(8,128)(2,1)} %all-gather.14.cloned.1.call-done), kind=kOutput, calls=%fused_computation.20 | convolution fusion | flops 14495514624 | bytes 28311552 | tf_op jit(solution)/shard_map/tpd,dk->tpk/dot_general | solution.py:119
  182.8 3.1 multiply_multiply_fusion.2
  185.9 3.0 copy-done.3
  188.9 5.8 slice.49
  194.7 5.8 slice.50
  200.4 3.0 slice.53
  203.5 3.1 slice.54
  206.5 6.5 %subtract_convert_fusion.1 = (bf16[384,4,4,64]{0,3,2,1:T(8,128)(2,1)S(1)}, bf16[384,4,4,64]{0,3,2,1:T(8,128)(2,1)S(1)}, bf16[384,4,4,64]{0,3,2,1:T(8,128)(2,1)S(1)}, bf16[384,4,4,64]{0,3,2,1:T(8,128)(2,1)S(1)}) fusion(f32[384,4,4,64]{0,3,2,1:T(8,128)} %slice.50, f32[384,4,4,64]{0,3,2,1:T(8,128)} %slice.49, f32[384,4,64]{0,2,1:T(8,128)} %get-tuple-element.34, ...), kind=kLoop, calls=%fused_computation.65 | loop fusion | flops 6291456 | bytes 10223616 | tf_op jit(solution)/shard_map/convert.2
  214.4 3.8 slice.80
  219.3 43.0 %fusion.95 = bf16[384,4,3072]{2,0,1:T(8,128)(2,1)} fusion(bf16[384,4,3072]{2,0,1:T(8,128)(2,1)} %all-gather.14.cloned.1.call-done, bf16[1,3072,3072]{2,1,0:T(8,128)(2,1)} %all-gather.24.cloned.1.call-done), kind=kOutput, calls=%fused_computation.11.clone.clone.1 | convolution fusion | flops 29033496576 | bytes 37748736 | tf_op jit(solution)/shard_map/tpd,dk->tpk/dot_general | solution.py:120
  262.4 37.8 %fusion.12 = f32[384,4,3072]{2,0,1:T(8,128)} fusion(bf16[1,3072,3072]{2,1,0:T(8,128)(2,1)} %all-gather.26.cloned.1.call-done, bf16[384,4,3072]{2,0,1:T(8,128)(2,1)} %fusion.95), kind=kOutput, calls=%fused_computation.13 | convolution fusion | flops 28991029248 | bytes 47185920 | tf_op jit(solution)/shard_map/tpk,kd->tpd/dot_general | solution.py:151
  300.2 50.6 %all-gather.16.cloned.1.call-done = bf16[1536,4,4,128]{0,3,2,1:T(8,128)(2,1)} async-done(((bf16[384,4,4,128]{0,3,2,1:T(8,128)(2,1)}), bf16[1536,4,4,128]{0,3,2,1:T(8,128)(2,1)}) %all-gather.16.cloned.1.call-update) | async-done | bytes 6291472 | tf_op jit(solution)/shard_map/all_gather | solution.py:131
  350.8 18.9 %fusion = (f32[4,4,384]{2,1,0:T(4,128)S(1)}, f32[4,4,384,1536]{3,2,1,0:T(8,128)}) fusion(f32[4,1536]{1,0:T(4,128)S(1)} %or_convert_fusion, bf16[1536,4,4,128]{0,3,2,1:T(8,128)(2,1)} %all-gather.16.cloned.1.call-done, bf16[384,4,4,64]{0,3,2,1:T(8,128)(2,1)S(1)} %get-tuple-element.21, bf16[384,4,4,64]{0,3,2,1:T(8,128)(2,1)S(1)} %get-tuple-element.20), kind=kOutput, calls=%fused_computation.1 | convolution fusion | flops 2447370240 | bytes 45662208 | tf_op jit(solution)/shard_map/sphe,tphe->phst/dot_general | solution.py:133
  369.7 96.1 %all-gather.20.cloned.1.call-done = bf16[1536,4,1,4,128]{0,4,3,2,1:T(8,128)(2,1)} async-done(((bf16[384,4,1,4,128]{0,4,3,2,1:T(8,128)(2,1)}), bf16[1536,4,1,4,128]{0,4,3,2,1:T(8,128)(2,1)}) %all-gather.20.cloned.1.call-update) | async-done | bytes 6291472 | tf_op jit(solution)/shard_map/all_gather | solution.py:132
  465.8 17.9 %fusion.42 = bf16[384,4,4,128]{0,3,2,1:T(8,128)(2,1)S(1)} fusion(f32[4,4,384,1536]{3,2,1,0:T(8,128)} %get-tuple-element.38, f32[4,1536]{1,0:T(4,128)S(1)} %or_convert_fusion, bf16[1536,4,1,4,128]{0,4,3,2,1:T(8,128)(2,1)} %all-gather.20.cloned.1.call-done, f32[384,4,4]{0,2,1:T(4,128)S(1)} %bitcast.144), kind=kOutput, calls=%fused_computation.51 | convolution fusion | flops 2445803520 | bytes 45662208 | tf_op jit(solution)/shard_map/phst,tphe->sphe/dot_general | solution.py:137
  483.8 12.4 %add_convert_fusion = bf16[384,4,3072]{2,0,1:T(8,128)(2,1)} fusion(f32[384,4,3072]{2,0,1:T(8,128)} %fusion.12, bf16[384,4,512]{0,2,1:T(8,128)(2,1)S(1)} %bitcast.147, bf16[1,512,3072]{2,1,0:T(8,128)(2,1)} %all-gather.22.cloned.1.call-done), kind=kOutput, calls=%fused_computation.17 | convolution fusion | flops 4841275392 | bytes 33030144 | tf_op jit(solution)/shard_map/tpk,kd->tpd/dot_general | solution.py:150
  497.1 92.2 %reduce-scatter.2.cloned.1.call-done = bf16[96,4,3072]{2,0,1:T(8,128)(2,1)} async-done(((bf16[384,4,3072]{2,0,1:T(8,128)(2,1)}), bf16[96,4,3072]{2,0,1:T(8,128)(2,1)}) %reduce-scatter.2.cloned.1.call-update) | async-done | bytes 2359312 | tf_op jit(solution)/shard_map/reduce_scatter | solution.py:148
  589.3 3.1 convert_reduce_fusion
  596.7 4.9 copy.38
  (69 shorter events, 16.0 us)
Async XLA Ops:
  7.2 586.0 %copy-start = (bf16[3072,64]{0,1:T(8,128)(2,1)S(1)}, bf16[3072,64]{0,1:T(8,128)(2,1)}, u32[]{:S(2)}) copy-start(bf16[3072,64]{0,1:T(8,128)(2,1)} %param.27) | copy-start | bytes 1179652
  7.2 58.4 %all-gather.18.cloned.1.call-start = ((), (), s32[]{:S(2)}) async-start(), calls=%async_computation.4 | async-start | bytes 14155776 | tf_op jit(solution)/shard_map/all_gather | solution.py:114
  13.9 0.8 copy-start.7
  14.0 41.4 %copy-start.1 = (bf16[1,96,4,3072]{3,2,1,0:T(4,128)(2,1)S(1)}, bf16[1,96,4,3072]{3,2,1,0:T(4,128)(2,1)}, u32[]{:S(2)}) copy-start(bf16[1,96,4,3072]{3,2,1,0:T(4,128)(2,1)} %param.14) | copy-start | bytes 7077892
  14.0 146.2 %all-gather.14.cloned.1.call-start = ((), (), s32[]{:S(2)}) async-start(), calls=%async_computation.1 | async-start | bytes 11796480 | tf_op jit(solution)/shard_map/all_gather | solution.py:109
  60.5 158.8 %all-gather.24.cloned.1.call-start = ((), (), s32[]{:S(2)}) async-start(), calls=%async_computation.7 | async-start | bytes 28311552 | tf_op jit(solution)/shard_map/all_gather | solution.py:115
  61.3 1.9 copy-start.11
  61.3 201.1 %all-gather.26.cloned.1.call-start = ((), (), s32[]{:S(2)}) async-start(), calls=%async_computation.8 | async-start | bytes 28311552 | tf_op jit(solution)/shard_map/all_gather | solution.py:147
  61.9 288.9 %all-gather.16.cloned.1.call-start = ((), (), s32[]{:S(2)}) async-start(), calls=%async_computation.2 | async-start | bytes 7864320 | tf_op jit(solution)/shard_map/all_gather | solution.py:131
  182.1 6.7 %copy-start.3 = (f32[384,4,3,4,128]{0,4,3,2,1:T(8,128)}, f32[384,4,3,4,128]{0,4,3,2,1:T(8,128)S(1)}, u32[]{:S(2)}) copy-start(f32[384,4,3,4,128]{0,4,3,2,1:T(8,128)S(1)} %fusion.19) | copy-start | bytes 28311556
  214.3 4.9 copy-start.10
  214.3 4.9 copy-start.12
  214.3 251.5 %all-gather.20.cloned.1.call-start = ((), (), s32[]{:S(2)}) async-start(), calls=%async_computation.5 | async-start | bytes 7864320 | tf_op jit(solution)/shard_map/all_gather | solution.py:132
  218.2 265.5 %all-gather.22.cloned.1.call-start = ((), (), s32[]{:S(2)}) async-start(), calls=%async_computation.6 | async-start | bytes 4718592 | tf_op jit(solution)/shard_map/all_gather | solution.py:146
  219.0 370.3 %reduce-scatter.2.cloned.1.call-start = ((), (), s32[]{:S(2)}) async-start(), calls=%async_computation.3 | async-start | bytes 11796480 | tf_op jit(solution)/shard_map/reduce_scatter | solution.py:148
  496.2 93.2 %copy-start.2 = (bf16[1,96,4,3072]{3,2,1,0:T(4,128)(2,1)S(1)}, bf16[1,96,4,3072]{3,2,1,0:T(4,128)(2,1)}, u32[]{:S(2)}) copy-start(bf16[1,96,4,3072]{3,2,1,0:T(4,128)(2,1)} %param.14) | copy-start | bytes 7077892
  496.2 93.2 %copy-start.5 = (f32[4,3072]{1,0:T(4,128)S(1)}, f32[4,3072]{1,0:T(4,128)}, u32[]{:S(2)}) copy-start(f32[4,3072]{1,0:T(4,128)} %get-tuple-element.30) | copy-start | bytes 147460
  589.3 3.9 copy-start.8
  589.3 3.9 copy-start.9
  592.4 2.1 copy-start.4
  593.2 8.3 %copy-start.6 = (f32[96,4,32]{0,2,1:T(8,128)S(1)}, f32[96,4,32]{0,2,1:T(8,128)}, u32[]{:S(2)}) copy-start(f32[96,4,32]{0,2,1:T(8,128)} %param.15) | copy-start | bytes 147460
  594.5 7.1 %collective-permute-start = (f32[96,4,32]{0,2,1:T(8,128)S(1)}, f32[96,4,32]{0,2,1:T(8,128)S(1)}, u32[]{:S(2)}, u32[]{:S(2)}) collective-permute-start(f32[96,4,32]{0,2,1:T(8,128)S(1)} %constant_dynamic-slice_fusion), channel_id=1, source_target_pairs={{0,16},{16,0},{1,17},{17,1},{2,18},{18,2},{3,19},{19,3},{4,20},{20... | collective-permute-start | bytes 147464 | tf_op jit(solution)/shard_map/ppermute | solution.py:20
Sparse Core Ops, SparseCore 0:
  14.1 24.2 all-gather.17
  60.7 99.4 all-gather.13
  161.7 34.1 all-gather.23
  197.4 34.9 all-gather.25
  234.3 116.3 all-gather.15
  352.2 113.5 all-gather.19
  467.4 10.5 all-gather.21
  496.3 92.9 reduce-scatter.1
where the time goes:
time: 614 us; the launch traced here: 609 us
  waiting for transfers between devices  336 us (55%)
  matrix products  158 us (26%)
  local copies, waits for them, and re-layouts  37.2 us (6%)
  blocking collectives  35.9 us (6%)
  other arithmetic  25.3 us (4%)
  between operations  16 us (3%)
    all_gather x1, waiting for transfers between devices, on_device(): values_piece = lax.all_gather(values, 'tok', axis=0, tiled=True)  96.1 us
    all_gather x1, waiting for transfers between devices, on_device(): tile_input = lax.all_gather(normed, 'mlp', axis=0, tiled=True)  94.6 us
    reduce_scatter x1, waiting for transfers between devices, on_device(): lax.psum_scatter((jnp.einsum('tpk,kd->tpd', attended, out_attn, preferred...  92.2 us
    all_gather x1, waiting for transfers between devices, on_device(): keys_piece = lax.all_gather(keys_rot, 'tok', axis=0, tiled=True)  50.6 us
    dot_general x1, matrix products, on_device(): jnp.einsum('tpd,dk->tpk', tile_input, pieces[1], preferred_element_type=j...  43 us
    dot_general x1, matrix products, on_device(): jnp.einsum('tpk,kd->tpd', activation, out_units, preferred_element_type=j...  37.8 us
    all_gather x1, blocking collectives, on_device(): modulation = lax.all_gather(mod_part, ('tok', 'mlp'), axis=1, tiled=True)  35.9 us
    dot_general x1, matrix products, on_device(): jnp.einsum('tpd,dk->tpk', tile_input, qkv_piece, preferred_element_type=j...  22 us
  transfers between devices with their start and end apart: 9, of which 4 were waited for; matrix products, arithmetic and copies ran while one was open for 31% of the time, Pallas kernels for 0%

commit v1 on v0

--- a/solution.py
+++ b/solution.py
@@ -3,12 +3,15 @@
 import jax
 import jax.numpy as jnp
 from jax import lax
+from jax.experimental import pallas as pl
+from jax.experimental.pallas import tpu as pltpu
 from jax.sharding import PartitionSpec as P
 
 LAYERS = 1
 SIDE = 32
 TXT = 512
 STEPS = 28
+PROMPTS = 4
 
 
 EPSILON = 1e-06
@@ -16,8 +19,8 @@
 TIME_SHIFT = 3.0
 
 
-def swapped(value, axis, apart):
-    return lax.ppermute(value, axis, [(i, i ^ 1 << apart) for i in range(lax.axis_size(axis))])
+def xor_swap(value, axis, apart):
+    return lax.ppermute(value, axis, [(i, i ^ apart) for i in range(lax.axis_size(axis))])
 
 
 def layer_norm(values):
@@ -92,7 +95,6 @@
     tok_index = lax.axis_index("tok")
     mlp_index = lax.axis_index("mlp")
     half_index = lax.axis_index("cfg")
-    first_half = half_index == 0
     stream = hidden[0]
     silu_vec = jax.nn.silu(vec[0]).astype(jnp.bfloat16)
     mod_part = jnp.dot(silu_vec, w_mod, preferred_element_type=jnp.float32)
@@ -167,23 +169,566 @@
         "rpd,dc->rpc", final_normed, w_final, preferred_element_type=jnp.float32
     )
     half_velocity = jnp.where((own_tokens >= TXT)[:, :, None], half_velocity, 0.0)
+    return guided(half_velocity, half_index, latents, step_index, guidance) + (stream[None],)
+
+
+VMEM_BYTES = 56 * 1024 * 1024
+TILE = 512
+SLOTS = 3
+ANY = pl.BlockSpec(memory_space=pl.ANY)
+VMEM = pl.BlockSpec(memory_space=pltpu.VMEM)
+SMEM = pl.BlockSpec(memory_space=pltpu.SMEM)
+
+
+def kernel_params():
+    return pltpu.CompilerParams(vmem_limit_bytes=VMEM_BYTES)
+
+
+def flip_by_bit(values, axis, bit):
+    return jnp.where(bit, jnp.flip(values, axis), values)
+
+
+def from_xor_order(values, axis, index, bits):
+    shape = values.shape
+    split = shape[:axis] + (2,) * bits + shape[axis + 1 :]
+    values = values.reshape(split)
+    for place in range(bits):
+        bit = (index >> (bits - 1 - place)) & 1
+        values = flip_by_bit(values, axis + place, bit == 1)
+    return values.reshape(shape)
+
+
+to_xor_order = from_xor_order
+
+
+def pick_kernel(place_ref, *refs):
+    count = len(refs) // 2
+    for j in range(count):
+        refs[count + j][...] = refs[j][0]
+
+
+def pick(place, states):
+    count, rows, width = states.shape
+    take = lambda j: lambda i, s: (s[0] ^ j, i, 0)
+    return pl.pallas_call(
+        pick_kernel,
+        out_shape=(jax.ShapeDtypeStruct((rows, width), states.dtype),) * count,
+        grid_spec=pltpu.PrefetchScalarGridSpec(
+            num_scalar_prefetch=1,
+            grid=(2,),
+            in_specs=[pl.BlockSpec((1, rows // 2, width), take(j)) for j in range(count)],
+            out_specs=[pl.BlockSpec((rows // 2, width), lambda i, s: (i, 0))] * count,
+        ),
+        compiler_params=kernel_params(),
+        cost_estimate=pl.CostEstimate(flops=0, bytes_accessed=4 * states.size, transcendentals=0),
+        name="pick",
+    )(place, *([states] * count))
+
+
+def sort_pairs_kernel(w_ref, sorter, out):
+    part = pl.program_id(0)
+    wide = sorter.shape[0]
+
+    @pl.when(part < 2)
+    def _():
+        for lo in range(0, out.shape[1], wide):
+            out[:, lo : lo + wide] = jnp.dot(
+                w_ref[0, :, lo : lo + wide], sorter[...], preferred_element_type=jnp.float32
+            ).astype(jnp.bfloat16)
+
+    @pl.when(part == 2)
+    def _():
+        out[...] = w_ref[0]
+
+
+def sort_pairs(weight, sorter):
+    parts, depth, cols = weight.shape
+    rows = depth // 2
+    return pl.pallas_call(
+        sort_pairs_kernel,
+        out_shape=jax.ShapeDtypeStruct((depth, parts * cols), weight.dtype),
+        grid=(parts, 2),
+        in_specs=[
+            pl.BlockSpec((1, rows, cols), lambda p, i: (p, i, 0)),
+            pl.BlockSpec(sorter.shape, lambda p, i: (0, 0)),
+        ],
+        out_specs=pl.BlockSpec((rows, cols), lambda p, i: (i, p)),
+        compiler_params=kernel_params(),
+        cost_estimate=pl.CostEstimate(
+            flops=4 * depth * cols * sorter.shape[0], bytes_accessed=4 * weight.size, transcendentals=0
+        ),
+        name="sort_pairs",
+    )(weight, sorter)
+
+
+def project_kernel(
+    half_ref,
+    shift,
+    scale,
+    cos_ref,
+    sin_ref,
+    gain,
+    x0,
+    x1,
+    x2,
+    x3,
+    wq_own,
+    wq_other,
+    wu_own,
+    wu_other,
+    q_out,
+    k_out,
+    v_out,
+    act_out,
+    landed,
+    normed,
+    held,
+    ready,
+    x_sem,
+    w_sem,
+    out_sem,
+):
+    half = half_ref[0]
+    depth = wq_own.shape[0]
+    head = gain.shape[1]
+    pieces = (x0, x1, x2, x3)
+    rows = x0.shape[0]
+    units = wu_own.shape[1] // TILE
+
+    def weights(own, other, column, slot):
+        return [
+            pltpu.make_async_copy(
+                ref.at[:, pl.ds(column, TILE)], held.at[slot, side], w_sem.at[slot, side]
+            )
+            for side, ref in enumerate((own, other))
+        ]
+
+    def result(out, column, slot):
+        return pltpu.make_async_copy(
+            ready.at[slot], out.at[:, pl.ds(column, TILE)], out_sem.at[slot]
+        )
+
+    loads = [pltpu.make_async_copy(ref, landed.at[i], x_sem.at[i]) for i, ref in enumerate(pieces)]
+    loads[0].start()
+    for copy in weights(wq_own, wq_other, 0, 0):
+        copy.start()
+    for load in loads[1:]:
+        load.start()
+    for part in (1, 2):
+        for copy in weights(wq_own, wq_other, part * TILE, part):
+            copy.start()
+
+    for index, load in enumerate(loads):
+        load.wait()
+        block = layer_norm(landed[index].astype(jnp.float32))
+        block = (block * scale[...] + shift[...]).astype(jnp.bfloat16)
+        normed[0, index * rows : (index + 1) * rows, :] = block[:, :depth]
+        normed[1, index * rows : (index + 1) * rows, :] = block[:, depth:]
+
+    def product(slot):
+        return jnp.dot(
+            normed[half], held[slot, 0], preferred_element_type=jnp.float32
+        ) + jnp.dot(normed[1 - half], held[slot, 1], preferred_element_type=jnp.float32)
+
+    for part, out in enumerate((q_out, k_out, v_out)):
+        for copy in weights(wq_own, wq_other, part * TILE, part):
+            copy.wait()
+        values = product(part)
+        if part == 2:
+            result(out, 0, 0).wait()
+            ready[0] = values.astype(jnp.bfloat16)
+        else:
+            for lo in range(0, TILE, head):
+                turned = rms_norm(values[:, lo : lo + head], gain[part : part + 1, :])
+                turned = turned * cos_ref[...] + pltpu.roll(turned, head // 2, 1) * sin_ref[...]
+                ready[part, :, lo : lo + head] = turned.astype(jnp.bfloat16)
+        result(out, 0, part % 2).start()
+        for copy in weights(wu_own, wu_other, part * TILE, part):
+            copy.start()
+
+    @pl.loop(0, units)
+    def _(index):
+        slot = lax.rem(index, SLOTS)
+        to = lax.rem(index + 1, 2)
+        column = pl.multiple_of(index * TILE, TILE)
+        for copy in weights(wu_own, wu_other, column, slot):
+            copy.wait()
+        values = jax.nn.gelu(product(slot), approximate=True).astype(jnp.bfloat16)
+        result(act_out, column, to).wait()
+        ready[to] = values
+        result(act_out, column, to).start()
+
+        @pl.when(index + SLOTS < units)
+        def _():
+            later = pl.multiple_of((index + SLOTS) * TILE, TILE)
+            for copy in weights(wu_own, wu_other, later, slot):
+                copy.start()
+
+    for slot in range(2):
+        result(act_out, 0, slot).wait()
+
+
+def project(half, pieces, shift, scale, cos_rows, sin_rows, gain, wq_own, wq_other, wu_own, wu_other):
+    rows = sum(piece.shape[0] for piece in pieces)
+    width = pieces[0].shape[1]
+    depth = wq_own.shape[0]
+    units = wu_own.shape[1]
+    head_out = jax.ShapeDtypeStruct((rows, TILE), jnp.bfloat16)
+    return pl.pallas_call(
+        project_kernel,
+        out_shape=(head_out, head_out, head_out, jax.ShapeDtypeStruct((rows, units), jnp.bfloat16)),
+        in_specs=[SMEM] + [VMEM] * 5 + [ANY] * 8,
+        out_specs=[ANY] * 4,
+        scratch_shapes=[
+            pltpu.VMEM((len(pieces), rows // len(pieces), width), jnp.bfloat16),
+            pltpu.VMEM((2, rows, depth), jnp.bfloat16),
+            pltpu.VMEM((SLOTS, 2, depth, TILE), jnp.bfloat16),
+            pltpu.VMEM((2, rows, TILE), jnp.bfloat16),
+            pltpu.SemaphoreType.DMA((len(pieces),)),
+            pltpu.SemaphoreType.DMA((SLOTS, 2)),
+            pltpu.SemaphoreType.DMA((2,)),
+        ],
+        compiler_params=kernel_params(),
+        cost_estimate=pl.CostEstimate(
+            flops=2 * rows * width * (3 * TILE + units),
+            bytes_accessed=2 * width * (3 * TILE + units) + 2 * rows * (width + 3 * TILE + units),
+            transcendentals=rows * units,
+        ),
+        name="project",
+    )(half, shift, scale, cos_rows, sin_rows, gain, *pieces, wq_own, wq_other, wu_own, wu_other)
+
+
+def combine_kernel(
+    half_ref,
+    bias,
+    q,
+    k0,
+    k1,
+    k2,
+    k3,
+    v0,
+    v1,
+    v2,
+    v3,
+    act,
+    wa_own,
+    wa_other,
+    wm_own,
+    wm_other,
+    p0,
+    p1,
+    p2,
+    p3,
+    attended,
+    units,
+    held_a,
+    held_m,
+    ready,
+    act_sem,
+    w_sem,
+    out_sem,
+):
+    half = half_ref[0]
+    keys, values, outs = (k0, k1, k2, k3), (v0, v1, v2, v3), (p0, p1, p2, p3)
+    rows = q.shape[0]
+    size = k0.shape[0]
+    piece = p0.shape[0]
+    head = 128
+    steps = wa_own.shape[1] // TILE
+
+    def weights(wa, wm, column, slot):
+        return [
+            pltpu.make_async_copy(wa.at[:, pl.ds(column, TILE)], held_a.at[slot], w_sem.at[slot, 0]),
+            pltpu.make_async_copy(wm.at[:, pl.ds(column, TILE)], held_m.at[slot], w_sem.at[slot, 1]),
+        ]
+
+    def results(column, slot):
+        return [
+            pltpu.make_async_copy(
+                ready.at[slot, pl.ds(i * piece, piece)],
+                out.at[:, pl.ds(column, TILE)],
+                out_sem.at[slot, i],
+            )
+            for i, out in enumerate(outs)
+        ]
+
+    load = pltpu.make_async_copy(act, units, act_sem)
+    load.start()
+    for slot in range(SLOTS):
+        for copy in weights(wa_own, wm_own, slot * TILE, slot):
+            copy.start()
+
+    @pl.loop(0, q.shape[1] // head)
+    def _(index):
+        lanes = pl.ds(pl.multiple_of(index * head, head), head)
+        total = jnp.zeros((rows, 1), jnp.float32)
+        numerator = jnp.zeros((rows, head), jnp.float32)
+        for part in range(len(keys)):
+            scores = lax.dot_general(
+                q[:, lanes],
+                keys[part][:, lanes],
+                (((1,), (1,)), ((), ())),
+                preferred_element_type=jnp.float32,
+            )
+            soft = jnp.exp(
+                scores * (1.0 / math.sqrt(head)) + bias[:, part * size : (part + 1) * size]
+            )
+            total += jnp.sum(soft, axis=-1, keepdims=True)
+            numerator += jnp.dot(
+                soft.astype(jnp.bfloat16), values[part][:, lanes], preferred_element_type=jnp.float32
+            )
+        attended[:, lanes] = (numerator / total).astype(jnp.bfloat16)
+
+    load.wait()
+
+    def write(index, slot, column, first, wa, wm):
+        for copy in weights(wa, wm, 0, slot):
+            copy.wait()
+        partial = jnp.dot(attended[...], held_a[slot], preferred_element_type=jnp.float32)
+        partial += jnp.dot(units[...], held_m[slot], preferred_element_type=jnp.float32)
+        to = lax.rem(index, 2)
+
+        @pl.when(index >= 2)
+        def _():
+            for copy in results(0, to):
+                copy.wait()
+
+        ready[to] = partial.astype(jnp.bfloat16)
+        for copy in results(column, to):
+            copy.start()
+
+    @pl.loop(0, 2 * steps)
+    def _(index):
+        slot = lax.rem(index, SLOTS)
+        place = lax.rem(index + steps * half, 2 * steps)
+        write(index, slot, pl.multiple_of(place * TILE, TILE), 0, wa_own, wm_own)
+
+        @pl.when(index + SLOTS < 2 * steps)
+        def _():
+            later = pl.multiple_of((index + SLOTS - steps) * TILE, TILE)
+            for copy in weights(wa_other, wm_other, later, slot):
+                copy.start()
+
+    for slot in range(2):
+        for copy in results(0, slot):
+            copy.wait()
+
+
+def combine(half, bias, q, keys, values, act, wa_own, wa_other, wm_own, wm_other):
+    rows, heads = q.shape
+    units = act.shape[1]
+    slots = bias.shape[1]
+    half_cols = wa_own.shape[1]
+    assert half_cols == SLOTS * TILE
+    pieces = len(keys)
+    part = jax.ShapeDtypeStruct((rows // pieces, 2 * half_cols), jnp.bfloat16)
+    return pl.pallas_call(
+        combine_kernel,
+        out_shape=(part,) * pieces,
+        in_specs=[SMEM] + [VMEM] * (2 + 2 * pieces) + [ANY] * 5,
+        out_specs=[ANY] * pieces,
+        scratch_shapes=[
+            pltpu.VMEM((rows, heads), jnp.bfloat16),
+            pltpu.VMEM((rows, units), jnp.bfloat16),
+            pltpu.VMEM((SLOTS, heads, TILE), jnp.bfloat16),
+            pltpu.VMEM((SLOTS, units, TILE), jnp.bfloat16),
+            pltpu.VMEM((2, rows, TILE), jnp.bfloat16),
+            pltpu.SemaphoreType.DMA,
+            pltpu.SemaphoreType.DMA((SLOTS, 2)),
+            pltpu.SemaphoreType.DMA((2, pieces)),
+        ],
+        compiler_params=kernel_params(),
+        cost_estimate=pl.CostEstimate(
+            flops=4 * rows * (heads + units) * half_cols + 4 * rows * slots * heads,
+            bytes_accessed=4 * (heads + units) * half_cols + 2 * rows * (heads + units + 2 * half_cols),
+            transcendentals=rows * slots * heads // 128,
+        ),
+        name="combine",
+    )(half, bias, q, *keys, *values, act, wa_own, wa_other, wm_own, wm_other)
+
+
+def finish_kernel(stream, shift, scale, w_final, velocity):
+    normed = (layer_norm(stream[...].astype(jnp.float32)) * scale[...] + shift[...]).astype(jnp.bfloat16)
+    velocity[...] = lax.dot_general(
+        normed, w_final[...], (((1,), (1,)), ((), ())), preferred_element_type=jnp.float32
+    )
+
+
+def finish(stream, shift, scale, w_final):
+    return pl.pallas_call(
+        finish_kernel,
+        out_shape=jax.ShapeDtypeStruct((stream.shape[0], w_final.shape[0]), jnp.float32),
+        compiler_params=kernel_params(),
+        cost_estimate=pl.CostEstimate(
+            flops=2 * stream.size * w_final.shape[0], bytes_accessed=2 * stream.size, transcendentals=0
+        ),
+        name="finish",
+    )(stream, shift, scale, w_final)
+
+
+def after(values, *done):
+    return lax.optimization_barrier((values, *done))[0]
+
+
+def by_prompt(
+    hidden,
+    latents,
+    vec,
+    slot_token,
+    text_len,
+    step_index,
+    guidance,
+    w_mod,
+    w_qkv,
+    w_mlp_in,
+    qk_gain,
+    w_attn_out,
+    w_mlp_out,
+    w_final,
+):
+    rows_dev, prompts, model_width = hidden.shape[1:]
+    head_size = qk_gain.shape[-1]
+    tok_index = lax.axis_index("tok")
+    mlp_index = lax.axis_index("mlp")
+    half_index = lax.axis_index("cfg")
+    half = half_index[None].astype(jnp.int32)
+
+    sends = pick(tok_index[None].astype(jnp.int32), jnp.transpose(hidden[0], (1, 0, 2)))
+
+    silu_vec = jax.nn.silu(vec[0]).astype(jnp.bfloat16)
+    mod_part = jnp.dot(after(silu_vec, sends[0]), w_mod, preferred_element_type=jnp.float32)
+    pair_order = jnp.concatenate([jnp.arange(0, head_size, 2), jnp.arange(1, head_size, 2)])
+    sorter = (jnp.arange(head_size)[:, None] == pair_order[None, :]).astype(jnp.bfloat16)
+    sorter = jnp.kron(jnp.eye(2, dtype=jnp.bfloat16), sorter)
+    wq_own = sort_pairs(jnp.transpose(w_qkv[0], (1, 0, 2)), after(sorter, mod_part))
+    wu_own, wa_own, wm_own = w_mlp_in[0], w_attn_out[0], w_mlp_out[0]
+    wu_other = xor_swap(wu_own, "cfg", 1)
+    wq_other = xor_swap(after(wq_own, wu_other), "cfg", 1)
+    gain = qk_gain[0][:, pair_order]
+
+    states_0, states_1 = sends[0], xor_swap(sends[1], "tok", 1)
+    by_x, by_y = xor_swap(states_0, "mlp", 1), xor_swap(states_0, "mlp", 2)
+    mods = to_xor_order(mod_part, 0, tok_index, 2)
+    mods = jnp.stack([mods[0::2], xor_swap(mods[1::2], "tok", 1)], 1)
+    mods = jnp.concatenate([mods[0], xor_swap(after(mods[1], wq_own), "tok", 2)], 0)
+    mods = jnp.stack([mods, xor_swap(after(mods, by_x, by_y, states_1), "mlp", 1)], 1)
+    cut = rows_dev // 2
+    far_top, far_low = xor_swap(by_x[:cut], "mlp", 2), xor_swap(by_y[cut:], "mlp", 1)
+    mods = jnp.concatenate([mods, xor_swap(mods, "mlp", 2)], 1)
+    mods = from_xor_order(from_xor_order(mods, 1, mlp_index, 2), 0, tok_index, 2)
+    shift_mod, scale_mod, gate_mod, final_shift, final_scale = jnp.split(
+        mods.reshape(1, 5 * model_width), 5, 1
+    )
+    scale_mod = 1.0 + scale_mod
+    final_scale = 1.0 + final_scale
+    wm_other = xor_swap(after(wm_own, shift_mod), "cfg", 1)
+    wa_other = xor_swap(after(wa_own, wm_other), "cfg", 1)
+
+    tokens = lax.dynamic_index_in_dim(slot_token, tok_index, 0, keepdims=False)
+    tokens = tokens.reshape(prompts, 4, rows_dev)
+    tokens = from_xor_order(from_xor_order(tokens, 1, mlp_index, 2), 0, tok_index, 2)
+    cosine, sine_table = rope_table(tokens.reshape(-1), head_size, TXT, SIDE)
+    cosine = jnp.concatenate([cosine, cosine], 1).reshape(prompts, 4 * rows_dev, head_size)
+    sine_table = jnp.concatenate([-sine_table, sine_table], 1).reshape(cosine.shape)
+    own_len = lax.dynamic_index_in_dim(text_len[0], tok_index, 0, keepdims=False)
+    bias = jnp.where((tokens >= TXT) | (tokens < own_len), 0.0, -1e30).reshape(1, -1)
+
+    own, queries, keys, values, acts = [], [], [], [], []
+    done = (far_top, far_low, shift_mod)
+    for j in range(prompts):
+        if j == 0:
+            states, far = states_0, jnp.concatenate([far_top, far_low], 0)
+        else:
+            states = states_1 if j == 1 else xor_swap(after(sends[j], own[-1]), "tok", j)
+            send = after(states, *done)
+            by_x, by_y, far = [xor_swap(send, "mlp", k) for k in (1, 2, 3)]
+        own.append(states)
+        q, k, v, act = project(
+            half,
+            (states, by_x, by_y, far),
+            shift_mod,
+            scale_mod,
+            cosine[j],
+            sine_table[j],
+            gain,
+            wq_own,
+            wq_other,
+            wu_own,
+            wu_other,
+        )
+        queries.append(q)
+        keys.append(k)
+        values.append(v)
+        acts.append(act)
+        if j:
+            done = (queries[j - 1], by_x, by_y, far, wm_other if j == 1 else wa_other)
+
+    streams, moved, speeds = [None] * prompts, [None] * prompts, [None] * prompts
+    parts = [None] * prompts
+
+    def sum_up(j, *done):
+        p0, by_x, by_y, far = parts[j]
+        terms = [part.astype(jnp.float32) for part in (after(p0, *done), by_x, by_y, far)]
+        branch = (terms[0] + terms[1]) + (terms[2] + terms[3])
+        streams[j] = (own[j].astype(jnp.float32) + gate_mod * branch).astype(jnp.bfloat16)
+        moved[j] = xor_swap(streams[j], "tok", j) if j else streams[j]
+        speeds[j] = finish(streams[j], final_shift, final_scale, w_final.T)
+        if j:
+            speeds[j] = xor_swap(speeds[j], "tok", j)
+
+    done = ()
+    for j in reversed(range(prompts)):
+        p0, p1, p2, p3 = combine(
+            half,
+            bias,
+            after(queries[j], *done),
+            keys,
+            values,
+            acts[j],
+            wa_own,
+            wa_other,
+            wm_own,
+            wm_other,
+        )
+        parts[j] = (p0, xor_swap(p1, "mlp", 1), xor_swap(p2, "mlp", 2), xor_swap(p3, "mlp", 3))
+        if j + 2 < prompts:
+            sum_up(j + 2, p0, *([moved[j + 3]] if j + 3 < prompts else []))
+            done = (streams[j + 2],)
+    sum_up(1, streams[2])
+    sum_up(0, streams[1], moved[2])
+
+    streams = moved
+    stream = from_xor_order(jnp.stack(streams, 1), 1, tok_index, 2)
+    half_velocity = from_xor_order(jnp.stack(speeds, 1), 1, tok_index, 2)
+    own_first = (tok_index * 4 + mlp_index) * rows_dev
+    own_tokens = lax.dynamic_slice_in_dim(slot_token, own_first, rows_dev, 1).T
+    half_velocity = jnp.where((own_tokens >= TXT)[:, :, None], half_velocity, 0.0)
+    return guided(half_velocity, half_index, latents, step_index, guidance) + (stream[None],)
+
+
+def guided(half_velocity, half_index, latents, step_index, guidance):
     channel_half = latents.shape[2]
     own_part = lax.dynamic_slice_in_dim(half_velocity, half_index * channel_half, channel_half, 2)
     sent_part = lax.dynamic_slice_in_dim(
         half_velocity, (1 - half_index) * channel_half, channel_half, 2
     )
-    partner = swapped(sent_part, "cfg", 0)
+    partner = xor_swap(sent_part, "cfg", 1)
+    first_half = half_index == 0
     cond_part = jnp.where(first_half, own_part, partner)
     uncond_part = jnp.where(first_half, partner, own_part)
     velocity = uncond_part + guidance[0] * (cond_part - uncond_part)
     current = step_index[0].astype(jnp.float32)
     step_size = sigma_at(current + 1.0, STEPS) - sigma_at(current, STEPS)
-    return (velocity, latents + step_size * velocity, stream[None])
+    return (velocity, latents + step_size * velocity)
+
+
+def fits_by_prompt(mesh):
+    return mesh.shape["cfg"] == 2 and mesh.shape["tok"] == PROMPTS and mesh.shape["mlp"] == 4
 
 
 def solution(mesh):
     return jax.shard_map(
-        on_device,
+        by_prompt if fits_by_prompt(mesh) else on_device,
         mesh=mesh,
         in_specs=(
             P("cfg", ("tok", "mlp"), None, None),

time: 614 us -> 354 us (0.58)
  waiting for transfers between devices: 336 us -> 92.1 us
  Pallas kernels: 0 us -> 172 us
  matrix products: 158 us -> 4.37 us
  starting transfers between devices: 1.8 us -> 47.4 us
  blocking collectives: 35.9 us -> 0 us
  local copies, waits for them, and re-layouts: 37.2 us -> 14.7 us
  between operations: 16 us -> 3.22 us
  other arithmetic: 25.3 us -> 16.6 us
    all_gather x7 -> x0, waiting for transfers between devices: 241 us -> none  [the longest x1 96.1 us: on_device(): values_piece = lax.all_gather(values, 'tok', axis=0, tiled=True)]
    pallas_call x0 -> x14, Pallas kernels: none -> 172 us  [the longest x4 84.7 us: project(): pl.pallas_call(project_kernel, out_shape=(head_out, head_out, head_out, j...]
    dot_general x8 -> x1, matrix products: 158 us -> 4.37 us  [by_prompt(): jnp.dot(after(silu_vec, sends[0]), w_mod, preferred_element_type=jnp.floa...]
    reduce_scatter x1 -> x0, waiting for transfers between devices: 92.2 us -> none  [on_device(): lax.psum_scatter((jnp.einsum('tpk,kd->tpd', attended, out_attn, preferred...]
    ppermute x1 -> x43, waiting for transfers between devices: 0.01 us -> 92.1 us  [xor_swap(): lax.ppermute(value, axis, [(i, i ^ apart) for i in range(lax.axis_size(ax...]
    ppermute x1 -> x43, starting transfers between devices: 0.78 us -> 47.4 us  [xor_swap(): lax.ppermute(value, axis, [(i, i ^ apart) for i in range(lax.axis_size(ax...]
    all_gather x1 -> x0, blocking collectives: 35.9 us -> none  [on_device(): modulation = lax.all_gather(mod_part, ('tok', 'mlp'), axis=1, tiled=True)]
    slice x5 -> x4, local copies, waits for them, and re-layouts: 21.5 us -> 0.83 us  [the longest x1 0.75 us: by_prompt(): by_y[cut:]]
  transfers between devices with their start and end apart: 9 -> 43, of which waited for: 4 -> 13; matrix products, arithmetic and copies ran while one was open for 31% -> 10% of each run, Pallas kernels for 0% -> 38%
where the time goes in v1:
time: 354 us; the launch traced here: 350 us
  Pallas kernels  172 us (49%)
  waiting for transfers between devices  92.1 us (26%)
  starting transfers between devices  47.4 us (13%)
  other arithmetic  16.6 us (5%)
  local copies, waits for them, and re-layouts  14.7 us (4%)
  matrix products  4.37 us (1%)
    ppermute x43, waiting for transfers between devices, xor_swap(): lax.ppermute(value, axis, [(i, i ^ apart) for i in range(lax.axis_size(ax...  92.1 us
    pallas_call x4, Pallas kernels, project(): pl.pallas_call(project_kernel, out_shape=(head_out, head_out, head_out, j...  84.7 us
    pallas_call x4, Pallas kernels, combine(): pl.pallas_call(combine_kernel, out_shape=(part,) * pieces, in_specs=[SMEM...  67.4 us
    ppermute x43, starting transfers between devices, xor_swap(): lax.ppermute(value, axis, [(i, i ^ apart) for i in range(lax.axis_size(ax...  47.4 us
    pallas_call x4, Pallas kernels, finish(): pl.pallas_call(finish_kernel, out_shape=jax.ShapeDtypeStruct((stream.shap...  10.1 us
  transfers between devices with their start and end apart: 43, of which 13 were waited for; matrix products, arithmetic and copies ran while one was open for 10% of the time, Pallas kernels for 38%

profile of v1, /device:TPU:1, one launch (start us, length us, event | category | flops | bytes accessed | tf_op | source)
XLA Modules:
  0.0 350.1 jit_solution(13263371950946905583)
XLA Ops:
  0.8 3.8 %copy.33 = bf16[1,96,4,3072]{3,1,2,0:T(8,128)(2,1)} copy(bf16[1,96,4,3072]{3,2,1,0:T(4,128)(2,1)} %param.14) | data formatting | bytes 4718592 | tf_op args[0]
  4.5 2.7 pick.1
  11.2 4.4 %fusion.24 = f32[4,960]{1,0:T(4,128)S(1)} fusion(bf16[4,3072]{1,0:T(4,128)(2,1)S(1)} %fusion.12, bf16[3072,960]{0,1:T(8,128)(2,1)} %param.21), kind=kOutput, calls=%fused_computation.100 | convolution fusion | flops 23592960 | bytes 5938176 | tf_op jit(solution)/shard_map/dot_general | solution.py:599
  18.5 6.7 %sort_pairs.1.wq_own = bf16[1536,1536]{1,0:T(8,128)(2,1)} custom-call(bf16[3,1536,512]{2,1,0:T(8,128)(2,1)} %bitcast.84, bf16[256,256]{1,0:T(8,128)(2,1)} %bitcast.89), custom_call_target="tpu_custom_call" | custom-call | flops 805306368 | bytes 9437184 | tf_op jit(solution)/shard_map/sort_pairs/pallas_call | solution.py:247
  38.8 4.1 %collective-permute-start.16 = (bf16[3072,1536]{1,0:T(8,128)(2,1)}, bf16[3072,1536]{1,0:T(8,128)(2,1)}, u32[]{:S(2)}, u32[]{:S(2)}) collective-permute-start(bf16[3072,1536]{1,0:T(8,128)(2,1)} %bitcast.117), channel_id=1, source_target_pairs={{0,16},{16,0},{1,17},{17,1},{2,18},{18,2},{3,19},{19,3},{4,20},{20... | collective-permute-start | bytes 28311560 | tf_op jit(solution)/shard_map/ppermute | solution.py:23
  45.5 2.9 fusion
  62.4 18.5 %collective-permute-done.11.x0 = bf16[96,3072]{1,0:T(8,128)(2,1)S(1)} collective-permute-done((bf16[96,3072]{1,0:T(8,128)(2,1)}, bf16[96,3072]{1,0:T(8,128)(2,1)S(1)}, u32[]{:S(2)}, u32[]{:S(2)}) %collective-permute-start.11) | collective-permute-done | bytes 589856 | tf_op jit(solution)/shard_map/ppermute | solution.py:23
  83.1 2.8 collective-permute-start.12
  88.0 21.2 %project.4 = (bf16[384,512]{1,0:T(8,128)(2,1)}, bf16[384,512]{1,0:T(8,128)(2,1)}, bf16[384,512]{1,0:T(8,128)(2,1)}, bf16[384,3072]{1,0:T(8,128)(2,1)}) custom-call(s32[1]{0:T(128)} %bitcast.14.half_ref, f32[1,3072]{1,0:T(1,128)} %get-tuple-element.122.shift, f32[1,3072]{1,0:T(1,128)} %get-tuple-element.121.scale, f32[384,128]{1,0:T(8,128)} %get-tuple-element.135.cos_ref, ...), custom_call_target="tpu_custom_call" | custom-call | flops 10871635968 | bytes 34209792 | tf_op jit(solution)/shard_map/project/pallas_call | solution.py:377
  112.0 21.2 %project.5 = (bf16[384,512]{1,0:T(8,128)(2,1)}, bf16[384,512]{1,0:T(8,128)(2,1)}, bf16[384,512]{1,0:T(8,128)(2,1)}, bf16[384,3072]{1,0:T(8,128)(2,1)}) custom-call(s32[1]{0:T(128)} %bitcast.14.half_ref, f32[1,3072]{1,0:T(1,128)} %get-tuple-element.122.shift, f32[1,3072]{1,0:T(1,128)} %get-tuple-element.121.scale, f32[384,128]{1,0:T(8,128)} %get-tuple-element.136.cos_ref, ...), custom_call_target="tpu_custom_call" | custom-call | flops 10871635968 | bytes 34209792 | tf_op jit(solution)/shard_map/project/pallas_call | solution.py:377
  133.2 3.7 %collective-permute-done.19.x3 = bf16[96,3072]{1,0:T(8,128)(2,1)} collective-permute-done((bf16[96,3072]{1,0:T(8,128)(2,1)S(1)}, bf16[96,3072]{1,0:T(8,128)(2,1)}, u32[]{:S(2)}, u32[]{:S(2)}) %collective-permute-start.19) | collective-permute-done | bytes 589856 | tf_op jit(solution)/shard_map/ppermute | solution.py:23
  139.6 21.2 %project.7 = (bf16[384,512]{1,0:T(8,128)(2,1)}, bf16[384,512]{1,0:T(8,128)(2,1)}, bf16[384,512]{1,0:T(8,128)(2,1)}, bf16[384,3072]{1,0:T(8,128)(2,1)}) custom-call(s32[1]{0:T(128)} %bitcast.14.half_ref, f32[1,3072]{1,0:T(1,128)} %get-tuple-element.122.shift, f32[1,3072]{1,0:T(1,128)} %get-tuple-element.121.scale, f32[384,128]{1,0:T(8,128)} %get-tuple-element.138.cos_ref, ...), custom_call_target="tpu_custom_call" | custom-call | flops 10871635968 | bytes 34209792 | tf_op jit(solution)/shard_map/project/pallas_call | solution.py:377
  160.9 3.8 %collective-permute-done.23.x3 = bf16[96,3072]{1,0:T(8,128)(2,1)S(1)} collective-permute-done((bf16[96,3072]{1,0:T(8,128)(2,1)S(1)}, bf16[96,3072]{1,0:T(8,128)(2,1)S(1)}, u32[]{:S(2)}, u32[]{:S(2)}) %collective-permute-start.23) | collective-permute-done | bytes 589856 | tf_op jit(solution)/shard_map/ppermute | solution.py:23
  165.5 21.1 %project.6 = (bf16[384,512]{1,0:T(8,128)(2,1)}, bf16[384,512]{1,0:T(8,128)(2,1)}, bf16[384,512]{1,0:T(8,128)(2,1)}, bf16[384,3072]{1,0:T(8,128)(2,1)}) custom-call(s32[1]{0:T(128)} %bitcast.14.half_ref, f32[1,3072]{1,0:T(1,128)} %get-tuple-element.122.shift, f32[1,3072]{1,0:T(1,128)} %get-tuple-element.121.scale, f32[384,128]{1,0:T(8,128)} %get-tuple-element.137.cos_ref, ...), custom_call_target="tpu_custom_call" | custom-call | flops 10871635968 | bytes 34209792 | tf_op jit(solution)/shard_map/project/pallas_call | solution.py:377
  186.7 16.8 %combine.4 = (bf16[96,3072]{1,0:T(8,128)(2,1)}, bf16[96,3072]{1,0:T(8,128)(2,1)}, bf16[96,3072]{1,0:T(8,128)(2,1)}, bf16[96,3072]{1,0:T(8,128)(2,1)}) custom-call(s32[1]{0:T(128)} %bitcast.14.half_ref, f32[1,1536]{1,0:T(1,128)} %select_n.228.bias, bf16[384,512]{1,0:T(8,128)(2,1)} %get-tuple-element.74.q, bf16[384,512]{1,0:T(8,128)(2,1)} %get-tuple-element.75.k0, ...), custom_call_target="tpu_custom_call" | custom-call | flops 9663676416 | bytes 27131904 | tf_op jit(solution)/shard_map/combine/pallas_call | solution.py:525
  206.2 16.8 %combine.5 = (bf16[96,3072]{1,0:T(8,128)(2,1)}, bf16[96,3072]{1,0:T(8,128)(2,1)}, bf16[96,3072]{1,0:T(8,128)(2,1)}, bf16[96,3072]{1,0:T(8,128)(2,1)}) custom-call(s32[1]{0:T(128)} %bitcast.14.half_ref, f32[1,1536]{1,0:T(1,128)} %select_n.228.bias, bf16[384,512]{1,0:T(8,128)(2,1)} %get-tuple-element.69.q, bf16[384,512]{1,0:T(8,128)(2,1)} %get-tuple-element.75.k0, ...), custom_call_target="tpu_custom_call" | custom-call | flops 9663676416 | bytes 27131904 | tf_op jit(solution)/shard_map/combine/pallas_call | solution.py:525
  223.0 16.9 %combine.7 = (bf16[96,3072]{1,0:T(8,128)(2,1)}, bf16[96,3072]{1,0:T(8,128)(2,1)}, bf16[96,3072]{1,0:T(8,128)(2,1)}, bf16[96,3072]{1,0:T(8,128)(2,1)}) custom-call(s32[1]{0:T(128)} %bitcast.14.half_ref, f32[1,1536]{1,0:T(1,128)} %select_n.228.bias, bf16[384,512]{1,0:T(8,128)(2,1)} %get-tuple-element.94.q, bf16[384,512]{1,0:T(8,128)(2,1)} %get-tuple-element.75.k0, ...), custom_call_target="tpu_custom_call" | custom-call | flops 9663676416 | bytes 27131904 | tf_op jit(solution)/shard_map/combine/pallas_call | solution.py:525
  247.2 17.0 %combine.6 = (bf16[96,3072]{1,0:T(8,128)(2,1)}, bf16[96,3072]{1,0:T(8,128)(2,1)}, bf16[96,3072]{1,0:T(8,128)(2,1)}, bf16[96,3072]{1,0:T(8,128)(2,1)}) custom-call(s32[1]{0:T(128)} %bitcast.14.half_ref, f32[1,1536]{1,0:T(1,128)} %select_n.228.bias, bf16[384,512]{1,0:T(8,128)(2,1)} %get-tuple-element.91.q, bf16[384,512]{1,0:T(8,128)(2,1)} %get-tuple-element.75.k0, ...), custom_call_target="tpu_custom_call" | custom-call | flops 9663676416 | bytes 27131904 | tf_op jit(solution)/shard_map/combine/pallas_call | solution.py:525
  266.3 5.1 %collective-permute-done.29 = bf16[96,3072]{1,0:T(8,128)(2,1)S(1)} collective-permute-done((bf16[96,3072]{1,0:T(8,128)(2,1)}, bf16[96,3072]{1,0:T(8,128)(2,1)S(1)}, u32[]{:S(2)}, u32[]{:S(2)}) %collective-permute-start.29) | collective-permute-done | bytes 589856 | tf_op jit(solution)/shard_map/ppermute | solution.py:23
  278.4 18.1 %collective-permute-done.32 = bf16[96,3072]{1,0:T(8,128)(2,1)S(1)} collective-permute-done((bf16[96,3072]{1,0:T(8,128)(2,1)S(1)}, bf16[96,3072]{1,0:T(8,128)(2,1)S(1)}, u32[]{:S(2)}, u32[]{:S(2)}) %collective-permute-start.32) | collective-permute-done | bytes 589856 | tf_op jit(solution)/shard_map/ppermute | solution.py:23
  301.6 23.5 %collective-permute-done.34 = bf16[96,3072]{1,0:T(8,128)(2,1)S(1)} collective-permute-done((bf16[96,3072]{1,0:T(8,128)(2,1)}, bf16[96,3072]{1,0:T(8,128)(2,1)S(1)}, u32[]{:S(2)}, u32[]{:S(2)}) %collective-permute-start.34) | collective-permute-done | bytes 589856 | tf_op jit(solution)/shard_map/ppermute | solution.py:23
  331.4 7.4 %collective-permute-done.39 = f32[96,64]{1,0:T(8,128)S(1)} collective-permute-done((f32[96,64]{1,0:T(8,128)S(1)}, f32[96,64]{1,0:T(8,128)S(1)}, u32[]{:S(2)}, u32[]{:S(2)}) %collective-permute-start.39) | collective-permute-done | bytes 24608 | tf_op jit(solution)/shard_map/ppermute | solution.py:23
  338.8 2.9 collective-permute-done.38
  345.7 3.2 copy.25
  (224 shorter events, 81.1 us)
Async XLA Ops:
  0.6 42.3 %collective-permute-start.9 = (bf16[1536,3072]{1,0:T(8,128)(2,1)}, bf16[1536,3072]{1,0:T(8,128)(2,1)}, u32[]{:S(2)}, u32[]{:S(2)}) collective-permute-start(bf16[1536,3072]{1,0:T(8,128)(2,1)} %bitcast.112), channel_id=1, source_target_pairs={{0,16},{16,0},{1,17},{17,1},{2,18},{18,2},{3,19},{19,3},{4,20},{20... | collective-permute-start | bytes 28311560 | tf_op jit(solution)/shard_map/ppermute | solution.py:23
  38.8 44.3 %collective-permute-start.16 = (bf16[3072,1536]{1,0:T(8,128)(2,1)}, bf16[3072,1536]{1,0:T(8,128)(2,1)}, u32[]{:S(2)}, u32[]{:S(2)}) collective-permute-start(bf16[3072,1536]{1,0:T(8,128)(2,1)} %bitcast.117), channel_id=1, source_target_pairs={{0,16},{16,0},{1,17},{17,1},{2,18},{18,2},{3,19},{19,3},{4,20},{20... | collective-permute-start | bytes 28311560 | tf_op jit(solution)/shard_map/ppermute | solution.py:23
  42.9 43.0 %collective-permute-start.10 = (bf16[1536,1536]{1,0:T(8,128)(2,1)}, bf16[1536,1536]{1,0:T(8,128)(2,1)}, u32[]{:S(2)}, u32[]{:S(2)}) collective-permute-start(bf16[1536,1536]{1,0:T(8,128)(2,1)} %sort_pairs.1.wq_own), channel_id=1, source_target_pairs={{0,16},{16,0},{1,17},{17,1},{2,18},{18,2},{3,19},{19,3},{4,20},{20... | collective-permute-start | bytes 14155784 | tf_op jit(solution)/shard_map/ppermute | solution.py:23
  53.3 27.6 %collective-permute-start.11 = (bf16[96,3072]{1,0:T(8,128)(2,1)}, bf16[96,3072]{1,0:T(8,128)(2,1)S(1)}, u32[]{:S(2)}, u32[]{:S(2)}) collective-permute-start(bf16[96,3072]{1,0:T(8,128)(2,1)} %get-tuple-element.66), channel_id=1, source_target_pairs={{0,8},{4,12},{8,0},{12,4},{1,9},{5,13},{9,1},{13,5},{2,10},{6,14},... | collective-permute-start | bytes 1769480 | tf_op jit(solution)/shard_map/ppermute | solution.py:23
  58.0 51.2 %collective-permute-start.13 = (bf16[96,3072]{1,0:T(8,128)(2,1)S(1)}, bf16[96,3072]{1,0:T(8,128)(2,1)S(1)}, u32[]{:S(2)}, u32[]{:S(2)}) collective-permute-start(bf16[96,3072]{1,0:T(8,128)(2,1)S(1)} %collective-permute-done.4.x0), channel_id=1, source_target_pairs={{0,1},{1,0},{2,3},{3,2},{4,5},{5,4},{6,7},{7,6},{8,9},{9,8},{10,11... | collective-permute-start | bytes 1769480 | tf_op jit(solution)/shard_map/ppermute | solution.py:23
  59.3 50.0 %collective-permute-start.14 = (bf16[96,3072]{1,0:T(8,128)(2,1)S(1)}, bf16[96,3072]{1,0:T(8,128)(2,1)S(1)}, u32[]{:S(2)}, u32[]{:S(2)}) collective-permute-start(bf16[96,3072]{1,0:T(8,128)(2,1)S(1)} %collective-permute-done.4.x0), channel_id=1, source_target_pairs={{0,2},{1,3},{2,0},{3,1},{4,6},{5,7},{6,4},{7,5},{8,10},{9,11},{10,... | collective-permute-start | bytes 1769480 | tf_op jit(solution)/shard_map/ppermute | solution.py:23
  81.0 28.3 %collective-permute-start.15 = (bf16[96,3072]{1,0:T(8,128)(2,1)S(1)}, bf16[96,3072]{1,0:T(8,128)(2,1)S(1)}, u32[]{:S(2)}, u32[]{:S(2)}) collective-permute-start(bf16[96,3072]{1,0:T(8,128)(2,1)S(1)} %collective-permute-done.4.x0), channel_id=1, source_target_pairs={{0,3},{1,2},{2,1},{3,0},{4,7},{5,6},{6,5},{7,4},{8,11},{9,10},{10,... | collective-permute-start | bytes 1769480 | tf_op jit(solution)/shard_map/ppermute | solution.py:23
  83.1 50.0 %collective-permute-start.12 = (bf16[96,3072]{1,0:T(8,128)(2,1)S(1)}, bf16[96,3072]{1,0:T(8,128)(2,1)S(1)}, u32[]{:S(2)}, u32[]{:S(2)}) collective-permute-start(bf16[96,3072]{1,0:T(8,128)(2,1)S(1)} %copy-done.26), channel_id=1, source_target_pairs={{0,12},{4,8},{8,4},{12,0},{1,13},{5,9},{9,5},{13,1},{2,14},{6,10},... | collective-permute-start | bytes 1769480 | tf_op jit(solution)/shard_map/ppermute | solution.py:23
  85.9 47.2 %collective-permute-start.20 = (bf16[512,1536]{1,0:T(8,128)(2,1)S(1)}, bf16[512,1536]{1,0:T(8,128)(2,1)S(1)}, u32[]{:S(2)}, u32[]{:S(2)}) collective-permute-start(bf16[512,1536]{1,0:T(8,128)(2,1)S(1)} %bitcast.126), channel_id=1, source_target_pairs={{0,16},{16,0},{1,17},{17,1},{2,18},{18,2},{3,19},{19,3},{4,20},{20... | collective-permute-start | bytes 4718600 | tf_op jit(solution)/shard_map/ppermute | solution.py:23
  109.7 27.2 %collective-permute-start.19 = (bf16[96,3072]{1,0:T(8,128)(2,1)S(1)}, bf16[96,3072]{1,0:T(8,128)(2,1)}, u32[]{:S(2)}, u32[]{:S(2)}) collective-permute-start(bf16[96,3072]{1,0:T(8,128)(2,1)S(1)} %collective-permute-done.11.x0), channel_id=1, source_target_pairs={{0,3},{1,2},{2,1},{3,0},{4,7},{5,6},{6,5},{7,4},{8,11},{9,10},{10,... | collective-permute-start | bytes 1769480 | tf_op jit(solution)/shard_map/ppermute | solution.py:23
  138.4 26.3 %collective-permute-start.23 = (bf16[96,3072]{1,0:T(8,128)(2,1)S(1)}, bf16[96,3072]{1,0:T(8,128)(2,1)S(1)}, u32[]{:S(2)}, u32[]{:S(2)}) collective-permute-start(bf16[96,3072]{1,0:T(8,128)(2,1)S(1)} %collective-permute-done.12.x0), channel_id=1, source_target_pairs={{0,3},{1,2},{2,1},{3,0},{4,7},{5,6},{6,5},{7,4},{8,11},{9,10},{10,... | collective-permute-start | bytes 1769480 | tf_op jit(solution)/shard_map/ppermute | solution.py:23
  203.5 37.7 %collective-permute-start.26 = (bf16[96,3072]{1,0:T(8,128)(2,1)}, bf16[96,3072]{1,0:T(8,128)(2,1)S(1)}, u32[]{:S(2)}, u32[]{:S(2)}) collective-permute-start(bf16[96,3072]{1,0:T(8,128)(2,1)} %get-tuple-element.90), channel_id=1, source_target_pairs={{0,3},{1,2},{2,1},{3,0},{4,7},{5,6},{6,5},{7,4},{8,11},{9,10},{10,... | collective-permute-start | bytes 1769480 | tf_op jit(solution)/shard_map/ppermute | solution.py:23
  204.2 38.3 %collective-permute-start.25 = (bf16[96,3072]{1,0:T(8,128)(2,1)}, bf16[96,3072]{1,0:T(8,128)(2,1)S(1)}, u32[]{:S(2)}, u32[]{:S(2)}) collective-permute-start(bf16[96,3072]{1,0:T(8,128)(2,1)} %get-tuple-element.89), channel_id=1, source_target_pairs={{0,2},{1,3},{2,0},{3,1},{4,6},{5,7},{6,4},{7,5},{8,10},{9,11},{10,... | collective-permute-start | bytes 1769480 | tf_op jit(solution)/shard_map/ppermute | solution.py:23
  204.8 38.5 %collective-permute-start.24 = (bf16[96,3072]{1,0:T(8,128)(2,1)}, bf16[96,3072]{1,0:T(8,128)(2,1)S(1)}, u32[]{:S(2)}, u32[]{:S(2)}) collective-permute-start(bf16[96,3072]{1,0:T(8,128)(2,1)} %get-tuple-element.88), channel_id=1, source_target_pairs={{0,1},{1,0},{2,3},{3,2},{4,5},{5,4},{6,7},{7,6},{8,9},{9,8},{10,11... | collective-permute-start | bytes 1769480 | tf_op jit(solution)/shard_map/ppermute | solution.py:23
  240.6 30.7 %collective-permute-start.29 = (bf16[96,3072]{1,0:T(8,128)(2,1)}, bf16[96,3072]{1,0:T(8,128)(2,1)S(1)}, u32[]{:S(2)}, u32[]{:S(2)}) collective-permute-start(bf16[96,3072]{1,0:T(8,128)(2,1)} %get-tuple-element.99), channel_id=1, source_target_pairs={{0,2},{1,3},{2,0},{3,1},{4,6},{5,7},{6,4},{7,5},{8,10},{9,11},{10,... | collective-permute-start | bytes 1769480 | tf_op jit(solution)/shard_map/ppermute | solution.py:23
  241.2 31.0 %collective-permute-start.28 = (bf16[96,3072]{1,0:T(8,128)(2,1)}, bf16[96,3072]{1,0:T(8,128)(2,1)S(1)}, u32[]{:S(2)}, u32[]{:S(2)}) collective-permute-start(bf16[96,3072]{1,0:T(8,128)(2,1)} %get-tuple-element.98), channel_id=1, source_target_pairs={{0,1},{1,0},{2,3},{3,2},{4,5},{5,4},{6,7},{7,6},{8,9},{9,8},{10,11... | collective-permute-start | bytes 1769480 | tf_op jit(solution)/shard_map/ppermute | solution.py:23
  242.6 35.9 %collective-permute-start.33 = (bf16[96,3072]{1,0:T(8,128)(2,1)}, bf16[96,3072]{1,0:T(8,128)(2,1)S(1)}, u32[]{:S(2)}, u32[]{:S(2)}) collective-permute-start(bf16[96,3072]{1,0:T(8,128)(2,1)} %get-tuple-element.104), channel_id=1, source_target_pairs={{0,3},{1,2},{2,1},{3,0},{4,7},{5,6},{6,5},{7,4},{8,11},{9,10},{10,... | collective-permute-start | bytes 1769480 | tf_op jit(solution)/shard_map/ppermute | solution.py:23
  264.2 32.3 %collective-permute-start.32 = (bf16[96,3072]{1,0:T(8,128)(2,1)S(1)}, bf16[96,3072]{1,0:T(8,128)(2,1)S(1)}, u32[]{:S(2)}, u32[]{:S(2)}) collective-permute-start(bf16[96,3072]{1,0:T(8,128)(2,1)S(1)} %copy-done.28), channel_id=1, source_target_pairs={{0,2},{1,3},{2,0},{3,1},{4,6},{5,7},{6,4},{7,5},{8,10},{9,11},{10,... | collective-permute-start | bytes 1769480 | tf_op jit(solution)/shard_map/ppermute | solution.py:23
  265.0 32.7 %collective-permute-start.31 = (bf16[96,3072]{1,0:T(8,128)(2,1)S(1)}, bf16[96,3072]{1,0:T(8,128)(2,1)S(1)}, u32[]{:S(2)}, u32[]{:S(2)}) collective-permute-start(bf16[96,3072]{1,0:T(8,128)(2,1)S(1)} %copy-done.27), channel_id=1, source_target_pairs={{0,1},{1,0},{2,3},{3,2},{4,5},{5,4},{6,7},{7,6},{8,9},{9,8},{10,11... | collective-permute-start | bytes 1769480 | tf_op jit(solution)/shard_map/ppermute | solution.py:23
  271.3 60.1 %collective-permute-start.40 = (f32[96,64]{1,0:T(8,128)S(1)}, f32[96,64]{1,0:T(8,128)S(1)}, u32[]{:S(2)}, u32[]{:S(2)}) collective-permute-start(f32[96,64]{1,0:T(8,128)S(1)} %copy-done.20), channel_id=1, source_target_pairs={{0,12},{4,8},{8,4},{12,0},{1,13},{5,9},{9,5},{13,1},{2,14},{6,10},... | collective-permute-start | bytes 73736 | tf_op jit(solution)/shard_map/ppermute | solution.py:23
  272.2 52.9 %collective-permute-start.37 = (bf16[96,3072]{1,0:T(8,128)(2,1)}, bf16[96,3072]{1,0:T(8,128)(2,1)S(1)}, u32[]{:S(2)}, u32[]{:S(2)}) collective-permute-start(bf16[96,3072]{1,0:T(8,128)(2,1)} %get-tuple-element.108), channel_id=1, source_target_pairs={{0,3},{1,2},{2,1},{3,0},{4,7},{5,6},{6,5},{7,4},{8,11},{9,10},{10,... | collective-permute-start | bytes 1769480 | tf_op jit(solution)/shard_map/ppermute | solution.py:23
  278.4 49.1 %collective-permute-start.36 = (bf16[96,3072]{1,0:T(8,128)(2,1)}, bf16[96,3072]{1,0:T(8,128)(2,1)S(1)}, u32[]{:S(2)}, u32[]{:S(2)}) collective-permute-start(bf16[96,3072]{1,0:T(8,128)(2,1)} %get-tuple-element.107), channel_id=1, source_target_pairs={{0,2},{1,3},{2,0},{3,1},{4,6},{5,7},{6,4},{7,5},{8,10},{9,11},{10,... | collective-permute-start | bytes 1769480 | tf_op jit(solution)/shard_map/ppermute | solution.py:23
  296.6 31.1 %collective-permute-start.35 = (bf16[96,3072]{1,0:T(8,128)(2,1)}, bf16[96,3072]{1,0:T(8,128)(2,1)S(1)}, u32[]{:S(2)}, u32[]{:S(2)}) collective-permute-start(bf16[96,3072]{1,0:T(8,128)(2,1)} %get-tuple-element.106), channel_id=1, source_target_pairs={{0,1},{1,0},{2,3},{3,2},{4,5},{5,4},{6,7},{7,6},{8,9},{9,8},{10,11... | collective-permute-start | bytes 1769480 | tf_op jit(solution)/shard_map/ppermute | solution.py:23
  297.6 27.4 %collective-permute-start.34 = (bf16[96,3072]{1,0:T(8,128)(2,1)}, bf16[96,3072]{1,0:T(8,128)(2,1)S(1)}, u32[]{:S(2)}, u32[]{:S(2)}) collective-permute-start(bf16[96,3072]{1,0:T(8,128)(2,1)} %add_convert_fusion.2.stream), channel_id=1, source_target_pairs={{0,8},{4,12},{8,0},{12,4},{1,9},{5,13},{9,1},{13,5},{2,10},{6,14},... | collective-permute-start | bytes 1769480 | tf_op jit(solution)/shard_map/ppermute | solution.py:23
  (57 other events, 896.5 us)

commit v2 on v1

--- a/solution.py
+++ b/solution.py
@@ -198,7 +198,9 @@
     return values.reshape(shape)
 
 
-to_xor_order = from_xor_order
+def xor_rows(count, index):
+    places = jnp.arange(count)
+    return (places[:, None] ^ index) == places[None, :]
 
 
 def pick_kernel(place_ref, *refs):
@@ -325,6 +327,9 @@
         normed[0, index * rows : (index + 1) * rows, :] = block[:, :depth]
         normed[1, index * rows : (index + 1) * rows, :] = block[:, depth:]
 
+    cosine = jnp.concatenate([cos_ref[...], cos_ref[...]], 1)
+    sine = jnp.concatenate([-sin_ref[...], sin_ref[...]], 1)
+
     def product(slot):
         return jnp.dot(
             normed[half], held[slot, 0], preferred_element_type=jnp.float32
@@ -340,7 +345,7 @@
         else:
             for lo in range(0, TILE, head):
                 turned = rms_norm(values[:, lo : lo + head], gain[part : part + 1, :])
-                turned = turned * cos_ref[...] + pltpu.roll(turned, head // 2, 1) * sin_ref[...]
+                turned = turned * cosine + pltpu.roll(turned, head // 2, 1) * sine
                 ready[part, :, lo : lo + head] = turned.astype(jnp.bfloat16)
         result(out, 0, part % 2).start()
         for copy in weights(wu_own, wu_other, part * TILE, part):
@@ -566,6 +571,10 @@
     )(stream, shift, scale, w_final)
 
 
+def add(left, right):
+    return (left.astype(jnp.float32) + right.astype(jnp.float32)).astype(jnp.bfloat16)
+
+
 def after(values, *done):
     return lax.optimization_barrier((values, *done))[0]
 
@@ -596,7 +605,23 @@
     sends = pick(tok_index[None].astype(jnp.int32), jnp.transpose(hidden[0], (1, 0, 2)))
 
     silu_vec = jax.nn.silu(vec[0]).astype(jnp.bfloat16)
-    mod_part = jnp.dot(after(silu_vec, sends[0]), w_mod, preferred_element_type=jnp.float32)
+    silu_vec = jnp.dot(
+        xor_rows(prompts, tok_index).astype(jnp.bfloat16), after(silu_vec, sends[0])
+    ).astype(jnp.bfloat16)
+    mod_part = jnp.dot(silu_vec, w_mod, preferred_element_type=jnp.float32)
+
+    tokens = lax.dynamic_index_in_dim(slot_token, tok_index, 0, keepdims=False).reshape(-1, rows_dev)
+    own_len = lax.dynamic_index_in_dim(text_len[0], tok_index, 0, keepdims=False)
+    order = xor_rows(4 * prompts, 4 * tok_index + mlp_index)
+    tokens = jnp.dot(
+        order.astype(jnp.float32), tokens.astype(jnp.float32), precision=lax.Precision.HIGHEST
+    )
+    tokens = jnp.round(tokens).astype(jnp.int32)
+    bias = jnp.where((tokens >= TXT) | (tokens < own_len), 0.0, -1e30).reshape(1, -1)
+    cosine, sine_table = rope_table(tokens.reshape(-1), head_size, TXT, SIDE)
+    cosine = cosine.reshape(prompts, 4 * rows_dev, -1)
+    sine_table = sine_table.reshape(cosine.shape)
+
     pair_order = jnp.concatenate([jnp.arange(0, head_size, 2), jnp.arange(1, head_size, 2)])
     sorter = (jnp.arange(head_size)[:, None] == pair_order[None, :]).astype(jnp.bfloat16)
     sorter = jnp.kron(jnp.eye(2, dtype=jnp.bfloat16), sorter)
@@ -608,14 +633,15 @@
 
     states_0, states_1 = sends[0], xor_swap(sends[1], "tok", 1)
     by_x, by_y = xor_swap(states_0, "mlp", 1), xor_swap(states_0, "mlp", 2)
-    mods = to_xor_order(mod_part, 0, tok_index, 2)
-    mods = jnp.stack([mods[0::2], xor_swap(mods[1::2], "tok", 1)], 1)
+    mods = jnp.stack([mod_part[0::2], xor_swap(mod_part[1::2], "tok", 1)], 1)
     mods = jnp.concatenate([mods[0], xor_swap(after(mods[1], wq_own), "tok", 2)], 0)
     mods = jnp.stack([mods, xor_swap(after(mods, by_x, by_y, states_1), "mlp", 1)], 1)
     cut = rows_dev // 2
     far_top, far_low = xor_swap(by_x[:cut], "mlp", 2), xor_swap(by_y[cut:], "mlp", 1)
-    mods = jnp.concatenate([mods, xor_swap(mods, "mlp", 2)], 1)
-    mods = from_xor_order(from_xor_order(mods, 1, mlp_index, 2), 0, tok_index, 2)
+    mods = jnp.concatenate([mods, xor_swap(after(mods, far_top, far_low), "mlp", 2)], 1)
+    mods = jnp.dot(
+        order.astype(jnp.float32), mods.reshape(order.shape[0], -1), precision=lax.Precision.HIGHEST
+    )
     shift_mod, scale_mod, gate_mod, final_shift, final_scale = jnp.split(
         mods.reshape(1, 5 * model_width), 5, 1
     )
@@ -623,15 +649,6 @@
     final_scale = 1.0 + final_scale
     wm_other = xor_swap(after(wm_own, shift_mod), "cfg", 1)
     wa_other = xor_swap(after(wa_own, wm_other), "cfg", 1)
-
-    tokens = lax.dynamic_index_in_dim(slot_token, tok_index, 0, keepdims=False)
-    tokens = tokens.reshape(prompts, 4, rows_dev)
-    tokens = from_xor_order(from_xor_order(tokens, 1, mlp_index, 2), 0, tok_index, 2)
-    cosine, sine_table = rope_table(tokens.reshape(-1), head_size, TXT, SIDE)
-    cosine = jnp.concatenate([cosine, cosine], 1).reshape(prompts, 4 * rows_dev, head_size)
-    sine_table = jnp.concatenate([-sine_table, sine_table], 1).reshape(cosine.shape)
-    own_len = lax.dynamic_index_in_dim(text_len[0], tok_index, 0, keepdims=False)
-    bias = jnp.where((tokens >= TXT) | (tokens < own_len), 0.0, -1e30).reshape(1, -1)
 
     own, queries, keys, values, acts = [], [], [], [], []
     done = (far_top, far_low, shift_mod)
@@ -639,7 +656,7 @@
         if j == 0:
             states, far = states_0, jnp.concatenate([far_top, far_low], 0)
         else:
-            states = states_1 if j == 1 else xor_swap(after(sends[j], own[-1]), "tok", j)
+            states = states_1 if j == 1 else xor_swap(after(sends[j], own[-1], *queries[: j - 2]), "tok", j)
             send = after(states, *done)
             by_x, by_y, far = [xor_swap(send, "mlp", k) for k in (1, 2, 3)]
         own.append(states)
@@ -666,19 +683,47 @@
     streams, moved, speeds = [None] * prompts, [None] * prompts, [None] * prompts
     parts = [None] * prompts
 
+    def straight(j):
+        p0, p1, p2, p3 = parts[j]
+        parts[j] = (p0, [xor_swap(p, "mlp", k) for k, p in ((1, p1), (2, p2), (3, p3))])
+
+    def first_step(j):
+        p0, p1, p2, p3 = parts[j]
+        if j == 0:
+            top, low = xor_swap(p3[:cut], "mlp", 1), xor_swap(p3[cut:], "mlp", 2)
+        elif j % 2:
+            top, low = xor_swap(p3, "mlp", 1), None
+        else:
+            top, low = None, xor_swap(p3, "mlp", 2)
+        parts[j] = (p0, p1, p2, top, low)
+
+    def second_step(j, *done):
+        p0, p1, p2, top, low = parts[j]
+        if j == 0:
+            p1 = jnp.concatenate([p1[:cut], add(p1[cut:], low)], 0)
+            p2 = jnp.concatenate([add(p2[:cut], top), p2[cut:]], 0)
+        elif j % 2:
+            p2 = add(p2, after(top, *done))
+        else:
+            p1 = add(p1, after(low, *done))
+        parts[j] = (p0, [xor_swap(p1, "mlp", 1), xor_swap(p2, "mlp", 2)])
+        return p2 if j % 2 else p1
+
     def sum_up(j, *done):
-        p0, by_x, by_y, far = parts[j]
-        terms = [part.astype(jnp.float32) for part in (after(p0, *done), by_x, by_y, far)]
-        branch = (terms[0] + terms[1]) + (terms[2] + terms[3])
+        p0, terms = parts[j]
+        branch = after(p0, *done).astype(jnp.float32)
+        for term in terms:
+            branch = branch + term.astype(jnp.float32)
         streams[j] = (own[j].astype(jnp.float32) + gate_mod * branch).astype(jnp.bfloat16)
         moved[j] = xor_swap(streams[j], "tok", j) if j else streams[j]
         speeds[j] = finish(streams[j], final_shift, final_scale, w_final.T)
         if j:
             speeds[j] = xor_swap(speeds[j], "tok", j)
+        return streams[j]
 
     done = ()
     for j in reversed(range(prompts)):
-        p0, p1, p2, p3 = combine(
+        parts[j] = combine(
             half,
             bias,
             after(queries[j], *done),
@@ -690,12 +735,16 @@
             wm_own,
             wm_other,
         )
-        parts[j] = (p0, xor_swap(p1, "mlp", 1), xor_swap(p2, "mlp", 2), xor_swap(p3, "mlp", 3))
+        mark, done = parts[j][0], ()
+        if j + 1 == prompts:
+            straight(j)
+            continue
+        first_step(j)
         if j + 2 < prompts:
-            sum_up(j + 2, p0, *([moved[j + 3]] if j + 3 < prompts else []))
-            done = (streams[j + 2],)
-    sum_up(1, streams[2])
-    sum_up(0, streams[1], moved[2])
+            done += (sum_up(j + 2, mark, *([moved[j + 3]] if j + 3 < prompts else [])),)
+            done += (second_step(j + 1, mark),)
+    done = (sum_up(1, streams[2]), second_step(0))
+    sum_up(0, *done, moved[2])
 
     streams = moved
     stream = from_xor_order(jnp.stack(streams, 1), 1, tok_index, 2)

time: 354 us -> 331 us (0.935)
  waiting for transfers between devices: 92.1 us -> 62.4 us
  starting transfers between devices: 47.4 us -> 55.4 us
    ppermute x43 -> x44, waiting for transfers between devices: 92.1 us -> 62.4 us  [xor_swap(): lax.ppermute(value, axis, [(i, i ^ apart) for i in range(lax.axis_size(ax...]
    ppermute x43 -> x44, starting transfers between devices: 47.4 us -> 55.4 us  [xor_swap(): lax.ppermute(value, axis, [(i, i ^ apart) for i in range(lax.axis_size(ax...]
  transfers between devices with their start and end apart: 43 -> 44, of which waited for: 13 -> 13; matrix products, arithmetic and copies ran while one was open for 10% -> 10% of each run, Pallas kernels for 38% -> 41%
where the time goes in v2:
time: 331 us; the launch traced here: 327 us
  Pallas kernels  172 us (52%)
  waiting for transfers between devices  62.4 us (19%)
  starting transfers between devices  55.4 us (17%)
  local copies, waits for them, and re-layouts  15.3 us (5%)
  other arithmetic  13.5 us (4%)
  matrix products  5.38 us (2%)
  between operations  3.32 us (1%)
    pallas_call x4, Pallas kernels, project(): pl.pallas_call(project_kernel, out_shape=(head_out, head_out, head_out, j...  85 us
    pallas_call x4, Pallas kernels, combine(): pl.pallas_call(combine_kernel, out_shape=(part,) * pieces, in_specs=[SMEM...  67.2 us
    ppermute x44, waiting for transfers between devices, xor_swap(): lax.ppermute(value, axis, [(i, i ^ apart) for i in range(lax.axis_size(ax...  62.4 us
    ppermute x44, starting transfers between devices, xor_swap(): lax.ppermute(value, axis, [(i, i ^ apart) for i in range(lax.axis_size(ax...  55.4 us
    pallas_call x4, Pallas kernels, finish(): pl.pallas_call(finish_kernel, out_shape=jax.ShapeDtypeStruct((stream.shap...  9.97 us
    pallas_call x1, Pallas kernels, sort_pairs(): pl.pallas_call(sort_pairs_kernel, out_shape=jax.ShapeDtypeStruct((depth,...  7.15 us
    unnamed x85, local copies, waits for them, and re-layouts  6.66 us
  transfers between devices with their start and end apart: 44, of which 13 were waited for; matrix products, arithmetic and copies ran while one was open for 10% of the time, Pallas kernels for 41%

profile of v2, /device:TPU:1, one launch (start us, length us, event | category | flops | bytes accessed | tf_op | source)
XLA Modules:
  0.0 327.4 jit_solution(7642570934493679961)
XLA Ops:
  0.8 3.8 %copy.38 = bf16[1,96,4,3072]{3,1,2,0:T(8,128)(2,1)} copy(bf16[1,96,4,3072]{3,2,1,0:T(4,128)(2,1)} %param.14) | data formatting | bytes 4718592 | tf_op args[0]
  11.2 4.4 %fusion = f32[4,960]{1,0:T(4,128)S(1)} fusion(bf16[3072,960]{0,1:T(8,128)(2,1)} %param.21, bf16[4,3072]{1,0:T(4,128)(2,1)S(1)} %fusion.9, s32[4]{0:T(128)S(1)} %iota_xor_fusion), kind=kOutput, calls=%fused_computation.11 | convolution fusion | flops 23691280 | bytes 5938192 | tf_op jit(solution)/shard_map/dot_general | solution.py:611
  18.2 7.2 %sort_pairs.1.wq_own = bf16[1536,1536]{1,0:T(8,128)(2,1)} custom-call(bf16[3,1536,512]{2,1,0:T(8,128)(2,1)} %bitcast.84, bf16[256,256]{1,0:T(8,128)(2,1)} %bitcast.89), custom_call_target="tpu_custom_call" | custom-call | flops 805306368 | bytes 9437184 | tf_op jit(solution)/shard_map/sort_pairs/pallas_call | solution.py:249
  38.4 3.6 %collective-permute-start.16 = (bf16[3072,1536]{1,0:T(8,128)(2,1)}, bf16[3072,1536]{1,0:T(8,128)(2,1)}, u32[]{:S(2)}, u32[]{:S(2)}) collective-permute-start(bf16[3072,1536]{1,0:T(8,128)(2,1)} %bitcast.115), channel_id=1, source_target_pairs={{0,16},{16,0},{1,17},{17,1},{2,18},{18,2},{3,19},{19,3},{4,20},{20... | collective-permute-start | bytes 28311560 | tf_op jit(solution)/shard_map/ppermute | solution.py:23
  48.8 2.9 fusion.4
  58.8 4.6 %collective-permute-done.10.wq_other = bf16[1536,1536]{1,0:T(8,128)(2,1)} collective-permute-done((bf16[1536,1536]{1,0:T(8,128)(2,1)}, bf16[1536,1536]{1,0:T(8,128)(2,1)}, u32[]{:S(2)}, u32[]{:S(2)}) %collective-permute-start.10) | collective-permute-done | bytes 4718624 | tf_op jit(solution)/shard_map/ppermute | solution.py:23
  63.8 21.3 %project.4 = (bf16[384,512]{1,0:T(8,128)(2,1)}, bf16[384,512]{1,0:T(8,128)(2,1)}, bf16[384,512]{1,0:T(8,128)(2,1)}, bf16[384,3072]{1,0:T(8,128)(2,1)}) custom-call(s32[1]{0:T(128)} %bitcast.13.half_ref, f32[1,3072]{1,0:T(1,128)} %get-tuple-element.130.shift, f32[1,3072]{1,0:T(1,128)} %get-tuple-element.129.scale, f32[384,64]{1,0:T(8,128)} %get-tuple-element.144.cos_ref, ...), custom_call_target="tpu_custom_call" | custom-call | flops 10871635968 | bytes 34209792 | tf_op jit(solution)/shard_map/project/pallas_call | solution.py:382
  90.7 21.2 %project.5 = (bf16[384,512]{1,0:T(8,128)(2,1)}, bf16[384,512]{1,0:T(8,128)(2,1)}, bf16[384,512]{1,0:T(8,128)(2,1)}, bf16[384,3072]{1,0:T(8,128)(2,1)}) custom-call(s32[1]{0:T(128)} %bitcast.13.half_ref, f32[1,3072]{1,0:T(1,128)} %get-tuple-element.130.shift, f32[1,3072]{1,0:T(1,128)} %get-tuple-element.129.scale, f32[384,64]{1,0:T(8,128)} %get-tuple-element.146.cos_ref, ...), custom_call_target="tpu_custom_call" | custom-call | flops 10871635968 | bytes 34209792 | tf_op jit(solution)/shard_map/project/pallas_call | solution.py:382
  115.5 21.2 %project.7 = (bf16[384,512]{1,0:T(8,128)(2,1)}, bf16[384,512]{1,0:T(8,128)(2,1)}, bf16[384,512]{1,0:T(8,128)(2,1)}, bf16[384,3072]{1,0:T(8,128)(2,1)}) custom-call(s32[1]{0:T(128)} %bitcast.13.half_ref, f32[1,3072]{1,0:T(1,128)} %get-tuple-element.130.shift, f32[1,3072]{1,0:T(1,128)} %get-tuple-element.129.scale, f32[384,64]{1,0:T(8,128)} %get-tuple-element.147.cos_ref, ...), custom_call_target="tpu_custom_call" | custom-call | flops 10871635968 | bytes 34209792 | tf_op jit(solution)/shard_map/project/pallas_call | solution.py:382
  136.8 3.0 collective-permute-done.23.x3
  140.7 21.2 %project.6 = (bf16[384,512]{1,0:T(8,128)(2,1)}, bf16[384,512]{1,0:T(8,128)(2,1)}, bf16[384,512]{1,0:T(8,128)(2,1)}, bf16[384,3072]{1,0:T(8,128)(2,1)}) custom-call(s32[1]{0:T(128)} %bitcast.13.half_ref, f32[1,3072]{1,0:T(1,128)} %get-tuple-element.130.shift, f32[1,3072]{1,0:T(1,128)} %get-tuple-element.129.scale, f32[384,64]{1,0:T(8,128)} %get-tuple-element.145.cos_ref, ...), custom_call_target="tpu_custom_call" | custom-call | flops 10871635968 | bytes 34209792 | tf_op jit(solution)/shard_map/project/pallas_call | solution.py:382
  161.9 16.8 %combine.4 = (bf16[96,3072]{1,0:T(8,128)(2,1)}, bf16[96,3072]{1,0:T(8,128)(2,1)}, bf16[96,3072]{1,0:T(8,128)(2,1)}, bf16[96,3072]{1,0:T(8,128)(2,1)}) custom-call(s32[1]{0:T(128)} %bitcast.13.half_ref, f32[1,1536]{1,0:T(1,128)} %reshape.230.bias, bf16[384,512]{1,0:T(8,128)(2,1)} %get-tuple-element.78.q, bf16[384,512]{1,0:T(8,128)(2,1)} %get-tuple-element.79.k0, ...), custom_call_target="tpu_custom_call" | custom-call | flops 9663676416 | bytes 27131904 | tf_op jit(solution)/shard_map/combine/pallas_call | solution.py:530
  181.4 16.8 %combine.6 = (bf16[96,3072]{1,0:T(8,128)(2,1)}, bf16[96,3072]{1,0:T(8,128)(2,1)}, bf16[96,3072]{1,0:T(8,128)(2,1)}, bf16[96,3072]{1,0:T(8,128)(2,1)}) custom-call(s32[1]{0:T(128)} %bitcast.13.half_ref, f32[1,1536]{1,0:T(1,128)} %reshape.230.bias, bf16[384,512]{1,0:T(8,128)(2,1)} %get-tuple-element.95.q, bf16[384,512]{1,0:T(8,128)(2,1)} %get-tuple-element.79.k0, ...), custom_call_target="tpu_custom_call" | custom-call | flops 9663676416 | bytes 27131904 | tf_op jit(solution)/shard_map/combine/pallas_call | solution.py:530
  199.0 16.8 %combine.5 = (bf16[96,3072]{1,0:T(8,128)(2,1)}, bf16[96,3072]{1,0:T(8,128)(2,1)}, bf16[96,3072]{1,0:T(8,128)(2,1)}, bf16[96,3072]{1,0:T(8,128)(2,1)}) custom-call(s32[1]{0:T(128)} %bitcast.13.half_ref, f32[1,1536]{1,0:T(1,128)} %reshape.230.bias, bf16[384,512]{1,0:T(8,128)(2,1)} %get-tuple-element.73.q, bf16[384,512]{1,0:T(8,128)(2,1)} %get-tuple-element.79.k0, ...), custom_call_target="tpu_custom_call" | custom-call | flops 9663676416 | bytes 27131904 | tf_op jit(solution)/shard_map/combine/pallas_call | solution.py:530
  216.6 3.7 %collective-permute-done.27 = bf16[96,3072]{1,0:T(8,128)(2,1)S(1)} collective-permute-done((bf16[96,3072]{1,0:T(8,128)(2,1)}, bf16[96,3072]{1,0:T(8,128)(2,1)S(1)}, u32[]{:S(2)}, u32[]{:S(2)}) %collective-permute-start.27) | collective-permute-done | bytes 589856 | tf_op jit(solution)/shard_map/ppermute | solution.py:23
  223.1 3.7 %collective-permute-start.28 = (bf16[96,3072]{1,0:T(8,128)(2,1)S(1)}, bf16[96,3072]{1,0:T(8,128)(2,1)S(1)}, u32[]{:S(2)}, u32[]{:S(2)}) collective-permute-start(bf16[96,3072]{1,0:T(8,128)(2,1)S(1)} %add_convert_fusion.5.stream), channel_id=1, source_target_pairs={{0,12},{4,8},{8,4},{12,0},{1,13},{5,9},{9,5},{13,1},{2,14},{6,10},... | collective-permute-start | bytes 1769480 | tf_op jit(solution)/shard_map/ppermute | solution.py:23
  226.8 16.8 %combine.7 = (bf16[96,3072]{1,0:T(8,128)(2,1)}, bf16[96,3072]{1,0:T(8,128)(2,1)}, bf16[96,3072]{1,0:T(8,128)(2,1)}, bf16[96,3072]{1,0:T(8,128)(2,1)}) custom-call(s32[1]{0:T(128)} %bitcast.13.half_ref, f32[1,1536]{1,0:T(1,128)} %reshape.230.bias, bf16[384,512]{1,0:T(8,128)(2,1)} %get-tuple-element.100.q, bf16[384,512]{1,0:T(8,128)(2,1)} %get-tuple-element.79.k0, ...), custom_call_target="tpu_custom_call" | custom-call | flops 9663676416 | bytes 27131904 | tf_op jit(solution)/shard_map/combine/pallas_call | solution.py:530
  249.4 16.8 %collective-permute-done.37 = bf16[48,3072]{1,0:T(8,128)(2,1)S(1)} collective-permute-done((bf16[48,3072]{1,0:T(8,128)(2,1)S(1)}, bf16[48,3072]{1,0:T(8,128)(2,1)S(1)}, u32[]{:S(2)}, u32[]{:S(2)}) %collective-permute-start.37) | collective-permute-done | bytes 294944 | tf_op jit(solution)/shard_map/ppermute | solution.py:23
  266.7 6.3 %collective-permute-done.34 = bf16[48,3072]{1,0:T(8,128)(2,1)S(1)} collective-permute-done((bf16[48,3072]{1,0:T(8,128)(2,1)S(1)}, bf16[48,3072]{1,0:T(8,128)(2,1)S(1)}, u32[]{:S(2)}, u32[]{:S(2)}) %collective-permute-start.34) | collective-permute-done | bytes 294944 | tf_op jit(solution)/shard_map/ppermute | solution.py:23
  273.0 4.2 %collective-permute-start.41 = (f32[96,64]{1,0:T(8,128)}, f32[96,64]{1,0:T(8,128)S(1)}, u32[]{:S(2)}, u32[]{:S(2)}) collective-permute-start(f32[96,64]{1,0:T(8,128)} %finish.7), channel_id=1, source_target_pairs={{0,12},{4,8},{8,4},{12,0},{1,13},{5,9},{9,5},{13,1},{2,14},{6,10},... | collective-permute-start | bytes 73736 | tf_op jit(solution)/shard_map/ppermute | solution.py:23
  282.5 7.1 %collective-permute-done.33 = bf16[96,3072]{1,0:T(8,128)(2,1)S(1)} collective-permute-done((bf16[96,3072]{1,0:T(8,128)(2,1)S(1)}, bf16[96,3072]{1,0:T(8,128)(2,1)S(1)}, u32[]{:S(2)}, u32[]{:S(2)}) %collective-permute-start.33) | collective-permute-done | bytes 589856 | tf_op jit(solution)/shard_map/ppermute | solution.py:23
  297.1 11.5 %collective-permute-done.35 = bf16[96,3072]{1,0:T(8,128)(2,1)S(1)} collective-permute-done((bf16[96,3072]{1,0:T(8,128)(2,1)S(1)}, bf16[96,3072]{1,0:T(8,128)(2,1)S(1)}, u32[]{:S(2)}, u32[]{:S(2)}) %collective-permute-start.35) | collective-permute-done | bytes 589856 | tf_op jit(solution)/shard_map/ppermute | solution.py:23
  316.6 4.9 %collective-permute-start.42 = (f32[96,4,32]{0,2,1:T(8,128)S(1)}, f32[96,4,32]{0,2,1:T(8,128)S(1)}, u32[]{:S(2)}, u32[]{:S(2)}) collective-permute-start(f32[96,4,32]{0,2,1:T(8,128)S(1)} %constant_dynamic-slice_fusion), channel_id=1, source_target_pairs={{0,16},{16,0},{1,17},{17,1},{2,18},{18,2},{3,19},{19,3},{4,20},{20... | collective-permute-start | bytes 147464 | tf_op jit(solution)/shard_map/ppermute | solution.py:23
  323.1 3.2 copy.30
  (228 shorter events, 81.0 us)
Async XLA Ops:
  0.6 41.4 %collective-permute-start.9 = (bf16[1536,3072]{1,0:T(8,128)(2,1)}, bf16[1536,3072]{1,0:T(8,128)(2,1)}, u32[]{:S(2)}, u32[]{:S(2)}) collective-permute-start(bf16[1536,3072]{1,0:T(8,128)(2,1)} %bitcast.110), channel_id=1, source_target_pairs={{0,16},{16,0},{1,17},{17,1},{2,18},{18,2},{3,19},{19,3},{4,20},{20... | collective-permute-start | bytes 28311560 | tf_op jit(solution)/shard_map/ppermute | solution.py:23
  53.0 32.1 %collective-permute-start.11 = (bf16[96,3072]{1,0:T(8,128)(2,1)S(1)}, bf16[96,3072]{1,0:T(8,128)(2,1)S(1)}, u32[]{:S(2)}, u32[]{:S(2)}) collective-permute-start(bf16[96,3072]{1,0:T(8,128)(2,1)S(1)} %copy-done.29), channel_id=1, source_target_pairs={{0,8},{4,12},{8,0},{12,4},{1,9},{5,13},{9,1},{13,5},{2,10},{6,14},... | collective-permute-start | bytes 1769480 | tf_op jit(solution)/shard_map/ppermute | solution.py:23
  56.1 29.0 %collective-permute-start.13 = (bf16[96,3072]{1,0:T(8,128)(2,1)S(1)}, bf16[96,3072]{1,0:T(8,128)(2,1)S(1)}, u32[]{:S(2)}, u32[]{:S(2)}) collective-permute-start(bf16[96,3072]{1,0:T(8,128)(2,1)S(1)} %collective-permute-done.4.x0), channel_id=1, source_target_pairs={{0,1},{1,0},{2,3},{3,2},{4,5},{5,4},{6,7},{7,6},{8,9},{9,8},{10,11... | collective-permute-start | bytes 1769480 | tf_op jit(solution)/shard_map/ppermute | solution.py:23
  56.8 28.4 %collective-permute-start.14 = (bf16[96,3072]{1,0:T(8,128)(2,1)S(1)}, bf16[96,3072]{1,0:T(8,128)(2,1)S(1)}, u32[]{:S(2)}, u32[]{:S(2)}) collective-permute-start(bf16[96,3072]{1,0:T(8,128)(2,1)S(1)} %collective-permute-done.4.x0), channel_id=1, source_target_pairs={{0,2},{1,3},{2,0},{3,1},{4,6},{5,7},{6,4},{7,5},{8,10},{9,11},{10,... | collective-permute-start | bytes 1769480 | tf_op jit(solution)/shard_map/ppermute | solution.py:23
  58.0 27.2 %collective-permute-start.15 = (bf16[96,3072]{1,0:T(8,128)(2,1)S(1)}, bf16[96,3072]{1,0:T(8,128)(2,1)S(1)}, u32[]{:S(2)}, u32[]{:S(2)}) collective-permute-start(bf16[96,3072]{1,0:T(8,128)(2,1)S(1)} %collective-permute-done.4.x0), channel_id=1, source_target_pairs={{0,3},{1,2},{2,1},{3,0},{4,7},{5,6},{6,5},{7,4},{8,11},{9,10},{10,... | collective-permute-start | bytes 1769480 | tf_op jit(solution)/shard_map/ppermute | solution.py:23
  63.4 48.5 %collective-permute-start.20 = (bf16[512,1536]{1,0:T(8,128)(2,1)S(1)}, bf16[512,1536]{1,0:T(8,128)(2,1)S(1)}, u32[]{:S(2)}, u32[]{:S(2)}) collective-permute-start(bf16[512,1536]{1,0:T(8,128)(2,1)S(1)} %bitcast.124), channel_id=1, source_target_pairs={{0,16},{16,0},{1,17},{17,1},{2,18},{18,2},{3,19},{19,3},{4,20},{20... | collective-permute-start | bytes 4718600 | tf_op jit(solution)/shard_map/ppermute | solution.py:23
  85.2 26.8 %collective-permute-start.17 = (bf16[96,3072]{1,0:T(8,128)(2,1)S(1)}, bf16[96,3072]{1,0:T(8,128)(2,1)S(1)}, u32[]{:S(2)}, u32[]{:S(2)}) collective-permute-start(bf16[96,3072]{1,0:T(8,128)(2,1)S(1)} %collective-permute-done.11.x0), channel_id=1, source_target_pairs={{0,1},{1,0},{2,3},{3,2},{4,5},{5,4},{6,7},{7,6},{8,9},{9,8},{10,11... | collective-permute-start | bytes 1769480 | tf_op jit(solution)/shard_map/ppermute | solution.py:23
  85.8 26.2 %collective-permute-start.18 = (bf16[96,3072]{1,0:T(8,128)(2,1)S(1)}, bf16[96,3072]{1,0:T(8,128)(2,1)S(1)}, u32[]{:S(2)}, u32[]{:S(2)}) collective-permute-start(bf16[96,3072]{1,0:T(8,128)(2,1)S(1)} %collective-permute-done.11.x0), channel_id=1, source_target_pairs={{0,2},{1,3},{2,0},{3,1},{4,6},{5,7},{6,4},{7,5},{8,10},{9,11},{10,... | collective-permute-start | bytes 1769480 | tf_op jit(solution)/shard_map/ppermute | solution.py:23
  87.1 25.5 %collective-permute-start.19 = (bf16[96,3072]{1,0:T(8,128)(2,1)S(1)}, bf16[96,3072]{1,0:T(8,128)(2,1)}, u32[]{:S(2)}, u32[]{:S(2)}) collective-permute-start(bf16[96,3072]{1,0:T(8,128)(2,1)S(1)} %collective-permute-done.11.x0), channel_id=1, source_target_pairs={{0,3},{1,2},{2,1},{3,0},{4,7},{5,6},{6,5},{7,4},{8,11},{9,10},{10,... | collective-permute-start | bytes 1769480 | tf_op jit(solution)/shard_map/ppermute | solution.py:23
  87.9 24.0 %collective-permute-start.12 = (bf16[96,3072]{1,0:T(8,128)(2,1)S(1)}, bf16[96,3072]{1,0:T(8,128)(2,1)S(1)}, u32[]{:S(2)}, u32[]{:S(2)}) collective-permute-start(bf16[96,3072]{1,0:T(8,128)(2,1)S(1)} %copy-done.28), channel_id=1, source_target_pairs={{0,12},{4,8},{8,4},{12,0},{1,13},{5,9},{9,5},{13,1},{2,14},{6,10},... | collective-permute-start | bytes 1769480 | tf_op jit(solution)/shard_map/ppermute | solution.py:23
  112.6 24.2 %collective-permute-start.21 = (bf16[96,3072]{1,0:T(8,128)(2,1)S(1)}, bf16[96,3072]{1,0:T(8,128)(2,1)S(1)}, u32[]{:S(2)}, u32[]{:S(2)}) collective-permute-start(bf16[96,3072]{1,0:T(8,128)(2,1)S(1)} %collective-permute-done.12.x0), channel_id=1, source_target_pairs={{0,1},{1,0},{2,3},{3,2},{4,5},{5,4},{6,7},{7,6},{8,9},{9,8},{10,11... | collective-permute-start | bytes 1769480 | tf_op jit(solution)/shard_map/ppermute | solution.py:23
  114.5 25.4 %collective-permute-start.23 = (bf16[96,3072]{1,0:T(8,128)(2,1)S(1)}, bf16[96,3072]{1,0:T(8,128)(2,1)S(1)}, u32[]{:S(2)}, u32[]{:S(2)}) collective-permute-start(bf16[96,3072]{1,0:T(8,128)(2,1)S(1)} %collective-permute-done.12.x0), channel_id=1, source_target_pairs={{0,3},{1,2},{2,1},{3,0},{4,7},{5,6},{6,5},{7,4},{8,11},{9,10},{10,... | collective-permute-start | bytes 1769480 | tf_op jit(solution)/shard_map/ppermute | solution.py:23
  178.7 42.4 %collective-permute-start.26 = (bf16[96,3072]{1,0:T(8,128)(2,1)}, bf16[96,3072]{1,0:T(8,128)(2,1)S(1)}, u32[]{:S(2)}, u32[]{:S(2)}) collective-permute-start(bf16[96,3072]{1,0:T(8,128)(2,1)} %get-tuple-element.94), channel_id=1, source_target_pairs={{0,3},{1,2},{2,1},{3,0},{4,7},{5,6},{6,5},{7,4},{8,11},{9,10},{10,... | collective-permute-start | bytes 1769480 | tf_op jit(solution)/shard_map/ppermute | solution.py:23
  180.6 41.4 %collective-permute-start.25 = (bf16[96,3072]{1,0:T(8,128)(2,1)}, bf16[96,3072]{1,0:T(8,128)(2,1)S(1)}, u32[]{:S(2)}, u32[]{:S(2)}) collective-permute-start(bf16[96,3072]{1,0:T(8,128)(2,1)} %get-tuple-element.93), channel_id=1, source_target_pairs={{0,2},{1,3},{2,0},{3,1},{4,6},{5,7},{6,4},{7,5},{8,10},{9,11},{10,... | collective-permute-start | bytes 1769480 | tf_op jit(solution)/shard_map/ppermute | solution.py:23
  180.6 42.0 %collective-permute-start.24 = (bf16[96,3072]{1,0:T(8,128)(2,1)}, bf16[96,3072]{1,0:T(8,128)(2,1)S(1)}, u32[]{:S(2)}, u32[]{:S(2)}) collective-permute-start(bf16[96,3072]{1,0:T(8,128)(2,1)} %get-tuple-element.92), channel_id=1, source_target_pairs={{0,1},{1,0},{2,3},{3,2},{4,5},{5,4},{6,7},{7,6},{8,9},{9,8},{10,11... | collective-permute-start | bytes 1769480 | tf_op jit(solution)/shard_map/ppermute | solution.py:23
  215.8 62.2 %collective-permute-start.30 = (bf16[96,3072]{1,0:T(8,128)(2,1)S(1)}, bf16[96,3072]{1,0:T(8,128)(2,1)S(1)}, u32[]{:S(2)}, u32[]{:S(2)}) collective-permute-start(bf16[96,3072]{1,0:T(8,128)(2,1)S(1)} %copy-done.31), channel_id=1, source_target_pairs={{0,2},{1,3},{2,0},{3,1},{4,6},{5,7},{6,4},{7,5},{8,10},{9,11},{10,... | collective-permute-start | bytes 1769480 | tf_op jit(solution)/shard_map/ppermute | solution.py:23
  221.1 58.7 %collective-permute-start.31 = (bf16[96,3072]{1,0:T(8,128)(2,1)S(1)}, bf16[96,3072]{1,0:T(8,128)(2,1)S(1)}, u32[]{:S(2)}, u32[]{:S(2)}) collective-permute-start(bf16[96,3072]{1,0:T(8,128)(2,1)S(1)} %copy-done.30), channel_id=1, source_target_pairs={{0,1},{1,0},{2,3},{3,2},{4,5},{5,4},{6,7},{7,6},{8,9},{9,8},{10,11... | collective-permute-start | bytes 1769480 | tf_op jit(solution)/shard_map/ppermute | solution.py:23
  222.1 56.8 %collective-permute-start.29 = (bf16[96,3072]{1,0:T(8,128)(2,1)S(1)}, bf16[96,3072]{1,0:T(8,128)(2,1)S(1)}, u32[]{:S(2)}, u32[]{:S(2)}) collective-permute-start(bf16[96,3072]{1,0:T(8,128)(2,1)S(1)} %add_convert_fusion.4), channel_id=1, source_target_pairs={{0,1},{1,0},{2,3},{3,2},{4,5},{5,4},{6,7},{7,6},{8,9},{9,8},{10,11... | collective-permute-start | bytes 1769480 | tf_op jit(solution)/shard_map/ppermute | solution.py:23
  223.1 54.2 %collective-permute-start.28 = (bf16[96,3072]{1,0:T(8,128)(2,1)S(1)}, bf16[96,3072]{1,0:T(8,128)(2,1)S(1)}, u32[]{:S(2)}, u32[]{:S(2)}) collective-permute-start(bf16[96,3072]{1,0:T(8,128)(2,1)S(1)} %add_convert_fusion.5.stream), channel_id=1, source_target_pairs={{0,12},{4,8},{8,4},{12,0},{1,13},{5,9},{9,5},{13,1},{2,14},{6,10},... | collective-permute-start | bytes 1769480 | tf_op jit(solution)/shard_map/ppermute | solution.py:23
  273.0 41.8 %collective-permute-start.41 = (f32[96,64]{1,0:T(8,128)}, f32[96,64]{1,0:T(8,128)S(1)}, u32[]{:S(2)}, u32[]{:S(2)}) collective-permute-start(f32[96,64]{1,0:T(8,128)} %finish.7), channel_id=1, source_target_pairs={{0,12},{4,8},{8,4},{12,0},{1,13},{5,9},{9,5},{13,1},{2,14},{6,10},... | collective-permute-start | bytes 73736 | tf_op jit(solution)/shard_map/ppermute | solution.py:23
  278.1 30.6 %collective-permute-start.38 = (bf16[96,3072]{1,0:T(8,128)(2,1)S(1)}, bf16[96,3072]{1,0:T(8,128)(2,1)}, u32[]{:S(2)}, u32[]{:S(2)}) collective-permute-start(bf16[96,3072]{1,0:T(8,128)(2,1)S(1)} %pad_maximum_fusion.3), channel_id=1, source_target_pairs={{0,2},{1,3},{2,0},{3,1},{4,6},{5,7},{6,4},{7,5},{8,10},{9,11},{10,... | collective-permute-start | bytes 1769480 | tf_op jit(solution)/shard_map/ppermute | solution.py:23
  278.9 31.0 %collective-permute-start.36 = (bf16[96,3072]{1,0:T(8,128)(2,1)S(1)}, bf16[96,3072]{1,0:T(8,128)(2,1)}, u32[]{:S(2)}, u32[]{:S(2)}) collective-permute-start(bf16[96,3072]{1,0:T(8,128)(2,1)S(1)} %pad_maximum_fusion.2), channel_id=1, source_target_pairs={{0,1},{1,0},{2,3},{3,2},{4,5},{5,4},{6,7},{7,6},{8,9},{9,8},{10,11... | collective-permute-start | bytes 1769480 | tf_op jit(solution)/shard_map/ppermute | solution.py:23
  279.8 28.8 %collective-permute-start.35 = (bf16[96,3072]{1,0:T(8,128)(2,1)S(1)}, bf16[96,3072]{1,0:T(8,128)(2,1)S(1)}, u32[]{:S(2)}, u32[]{:S(2)}) collective-permute-start(bf16[96,3072]{1,0:T(8,128)(2,1)S(1)} %add_convert_fusion.3.stream), channel_id=1, source_target_pairs={{0,8},{4,12},{8,0},{12,4},{1,9},{5,13},{9,1},{13,5},{2,10},{6,14},... | collective-permute-start | bytes 1769480 | tf_op jit(solution)/shard_map/ppermute | solution.py:23
  290.1 31.5 %collective-permute-start.43 = (bf16[96,3072]{1,0:T(8,128)(2,1)S(1)}, bf16[96,3072]{1,0:T(8,128)(2,1)S(1)}, u32[]{:S(2)}, u32[]{:S(2)}) collective-permute-start(bf16[96,3072]{1,0:T(8,128)(2,1)S(1)} %add_convert_fusion.1.stream), channel_id=1, source_target_pairs={{0,4},{4,0},{8,12},{12,8},{1,5},{5,1},{9,13},{13,9},{2,6},{6,2},{1... | collective-permute-start | bytes 1769480 | tf_op jit(solution)/shard_map/ppermute | solution.py:23
  (60 other events, 723.3 us)
